TPU v7x, 32 devices: a whole 2x2x4 slice. The times are simulated.
32 devices in a mesh: fsdp: 4 (over z), context: 2 (over y), tensor: 4 (over x, core).
Axes of the slice: x: 2, y: 2, z: 4, core: 2. Of those that a mesh axis runs over, the one named last changes fastest.
Arguments:
- tokens: bfloat16 [4, 2048, 1536], P('fsdp', ('context', 'tensor')), may hold values from -6 to 6
- cotangent: bfloat16 [4, 2048, 1536], P('fsdp', ('context', 'tensor')), may hold values from -6 to 6
- segment_ids: int32 [4, 2048], P('fsdp'), may hold values from 0 to 511, as said below
- w_query: bfloat16 [1536, 1536], P(('fsdp', 'context'), 'tensor'), may hold values from -0.15625 to 0.15625
- w_keyval: bfloat16 [1536, 256], P(('fsdp', 'context', 'tensor')), may hold values from -0.15625 to 0.15625
- w_out: bfloat16 [1536, 1536], P('tensor', ('fsdp', 'context')), may hold values from -0.875 to 0.875
- w_gate: bfloat16 [1536, 4608], P(('fsdp', 'context'), 'tensor'), may hold values from -0.15625 to 0.15625
- w_up: bfloat16 [1536, 4608], P(('fsdp', 'context'), 'tensor'), may hold values from -0.15625 to 0.15625
- contract_factor: bfloat16 [4608, 1536], P('tensor', ('fsdp', 'context')), may hold values from -0.09375 to 0.09375
- norm_gains: bfloat16 [2, 1536], P(None, ('fsdp', 'context', 'tensor')), may hold values from 0.099609375 to 1.8984375
Outputs:
- output: bfloat16 [4, 2048, 1536], P('fsdp', ('context', 'tensor'))
- input_grad: float32 [4, 2048, 1536], P('fsdp', ('context', 'tensor'))
- grad_query: float32 [1536, 1536], P(('fsdp', 'context'), 'tensor')
- grad_keyval: float32 [1536, 256], P(('fsdp', 'context', 'tensor'))
- grad_out: float32 [1536, 1536], P('tensor', ('fsdp', 'context'))
- grad_gate: float32 [1536, 4608], P(('fsdp', 'context'), 'tensor')
- grad_up: float32 [1536, 4608], P(('fsdp', 'context'), 'tensor')
- grad_down: float32 [4608, 1536], P('tensor', ('fsdp', 'context'))
- grad_gains: float32 [2, 1536], P(None, ('fsdp', 'context', 'tensor'))
Inputs may be any that keep to these rules, and one draw needn't show every extreme that they name: `segment_ids`: along each sequence the ids start at 0 and rise by one where a new document begins; every document but a sequence's last holds 4 tokens or more and up to 2048; one of the sequences is a single document, and another is cut into documents of 4 tokens each.
All inputs are finite; a program needn't handle non-finite values.
Results may differ from a plain program's by a relative error of at most 0.015.
Values may be sent and summed in bfloat16 or wider, within the bound.
No kernel may reach another device: no remote copies, remote signals or barrier semaphores. Data moves between devices by JAX's collectives and lax.ppermute only.
A program may use at most 192 MiB of HBM per device.

v0:
```python
import jax
import jax.numpy as jnp
from jax import lax
from jax.sharding import PartitionSpec as P

HEAD_DIM = 128
WINDOW = 1024


EPSILON = 1e-06


def from_behind(value, axis, steps):
    count = lax.axis_size(axis)
    leading, last = (max(0, -steps), min(count, count - steps))
    return lax.ppermute(value, axis, [(source, source + steps) for source in range(leading, last)])


def rms_inverse(values):
    return lax.rsqrt(jnp.mean(values * values, axis=-1, keepdims=True) + EPSILON)


def norm_backward(grad_normed, values, inv_rms, gain_row):
    scaled = grad_normed * gain_row
    inner_sum = jnp.mean(scaled * values, axis=-1, keepdims=True)
    return inv_rms * scaled - values * (inv_rms * inv_rms * inv_rms) * inner_sum


def local(
    tokens,
    cotangent,
    segment_ids,
    w_query,
    w_keyval,
    w_out,
    w_gate,
    w_up,
    contract_factor,
    norm_gains,
):
    seq_count = tokens.shape[0]
    tensor_count = lax.axis_size("tensor")
    own_rows = tokens.shape[1]
    shard_len = own_rows * tensor_count
    first_pos = lax.axis_index("context") * shard_len
    query_full, out_full, gate_weight_whole, up_weight_whole, contract_factor_entire = (
        lax.all_gather(w_query, ("fsdp", "context"), axis=0, tiled=True),
        lax.all_gather(w_out, ("fsdp", "context"), axis=1, tiled=True),
        lax.all_gather(w_gate, ("fsdp", "context"), axis=0, tiled=True),
        lax.all_gather(w_up, ("fsdp", "context"), axis=0, tiled=True),
        lax.all_gather(contract_factor, ("fsdp", "context"), axis=1, tiled=True),
    )
    keyvalue_weight_whole, gains_full = (
        lax.all_gather(w_keyval, ("fsdp", "context", "tensor"), axis=0, tiled=True),
        lax.all_gather(norm_gains, ("fsdp", "context", "tensor"), axis=1, tiled=True),
    )
    gain_one = gains_full[0].astype(jnp.float32)
    gain_two = gains_full[1].astype(jnp.float32)
    input_rows = tokens.astype(jnp.float32)
    inv_one = rms_inverse(input_rows)
    normed_one = (input_rows * inv_one * gain_one).astype(jnp.bfloat16)
    query_matrix, output_matrix = (query_full, out_full)
    attention_rows = lax.all_gather(normed_one, "tensor", axis=1, tiled=True)
    keyvals = jnp.einsum(
        "tve,ez->tvz", attention_rows, keyvalue_weight_whole, preferred_element_type=jnp.float32
    ).astype(jnp.bfloat16)
    groups_here = 1
    queries = jnp.einsum(
        "whn,nz->whz", attention_rows, query_matrix, preferred_element_type=jnp.float32
    ).astype(jnp.bfloat16)
    rows_here = attention_rows.shape[1]
    heads_here = queries.shape[2] // HEAD_DIM
    per_group = heads_here // groups_here
    earlier = from_behind(keyvals, "context", 1)
    both_keys = jnp.concatenate([earlier, keyvals], axis=1)
    seg_padded = jnp.concatenate(
        [jnp.full((seq_count, shard_len), -1, jnp.int32), segment_ids], axis=1
    )
    key_segs = lax.dynamic_slice_in_dim(seg_padded, first_pos, 2 * shard_len, 1)
    block_rows = min(512, rows_here)
    block_count = rows_here // block_rows
    key_rows = block_rows + WINDOW
    score_scale = HEAD_DIM ** (-0.5)
    tile_numbers = jnp.arange(seq_count * block_count, dtype=jnp.int32)

    def block_parts(block_index):
        seq_pos = block_index // block_count
        block_at = block_index % block_count
        first_token_offset = block_at * block_rows
        key_start = shard_len + first_token_offset - WINDOW
        query_blk = lax.dynamic_slice_in_dim(
            lax.dynamic_index_in_dim(queries, seq_pos, 0, False), first_token_offset, block_rows, 0
        )
        query_blk = query_blk.reshape(block_rows, groups_here, per_group, HEAD_DIM)
        kv_blk = lax.dynamic_slice_in_dim(
            lax.dynamic_index_in_dim(both_keys, seq_pos, 0, False), key_start, key_rows, 0
        )
        seg_row = lax.dynamic_index_in_dim(key_segs, seq_pos, 0, False)
        key_seg = lax.dynamic_slice_in_dim(seg_row, key_start, key_rows, 0)
        query_seg = lax.dynamic_slice_in_dim(seg_row, shard_len + first_token_offset, block_rows, 0)
        query_pos = first_token_offset + jnp.arange(block_rows, dtype=jnp.int32)
        key_pos = key_start - shard_len + jnp.arange(key_rows, dtype=jnp.int32)
        allowed = (
            (key_pos[None, :] <= query_pos[:, None])
            & (key_pos[None, :] > query_pos[:, None] - WINDOW)
            & (key_seg[None, :] == query_seg[:, None])
        )
        scores = (
            jnp.einsum(
                "qgpd,kd->gpqk", query_blk, kv_blk[:, :HEAD_DIM], preferred_element_type=jnp.float32
            )
            * score_scale
        )
        scores = jnp.where(allowed[None, None], scores, -1e30)
        return (query_blk, kv_blk, scores, seq_pos, key_start)

    def forward_block(block_index):
        query_blk, kv_blk, scores, seq_pos, key_start = block_parts(block_index)
        row_max = jnp.max(scores, axis=-1, keepdims=True)
        powers = jnp.exp(scores - row_max)
        row_sum = jnp.sum(powers, axis=-1, keepdims=True)
        attn_probs = (powers / row_sum).astype(jnp.bfloat16)
        mixed_out = jnp.einsum(
            "gpqk,kd->qgpd", attn_probs, kv_blk[:, HEAD_DIM:], preferred_element_type=jnp.float32
        )
        return (
            mixed_out.reshape(block_rows, heads_here * HEAD_DIM).astype(jnp.bfloat16),
            row_max[..., 0] + jnp.log(row_sum[..., 0]),
        )

    mixed_blocks, log_sums = lax.map(forward_block, tile_numbers)
    attention_head_rows = mixed_blocks.reshape(seq_count, rows_here, heads_here * HEAD_DIM)
    portion_output = jnp.einsum(
        "cxe,ew->cxw", attention_head_rows, output_matrix, preferred_element_type=jnp.float32
    )
    attn_add = lax.psum_scatter(portion_output, "tensor", scatter_dimension=1, tiled=True)
    middle = input_rows + attn_add
    inv_two = rms_inverse(middle)
    normed_two = (middle * inv_two * gain_two).astype(jnp.bfloat16)
    second_normed_whole, derivative_entire = (
        lax.all_gather(normed_two, "tensor", axis=1, tiled=True),
        lax.all_gather(cotangent, "tensor", axis=1, tiled=True),
    )
    gate_pre = jnp.einsum(
        "pha,ab->phb", second_normed_whole, gate_weight_whole, preferred_element_type=jnp.float32
    )
    up_preactivation = jnp.einsum(
        "pha,ab->phb", second_normed_whole, up_weight_whole, preferred_element_type=jnp.float32
    )
    activated, gelu_back = jax.vjp(lambda gate_in: jax.nn.gelu(gate_in, approximate=True), gate_pre)
    hidden_activation = (activated * up_preactivation).astype(jnp.bfloat16)
    feedforward_portion = jnp.einsum(
        "qgx,xr->qgr", hidden_activation, contract_factor_entire, preferred_element_type=jnp.float32
    )
    ffn_add = lax.psum_scatter(
        feedforward_portion.astype(jnp.bfloat16), "tensor", scatter_dimension=1, tiled=True
    ).astype(jnp.float32)
    output = (middle + ffn_add).astype(jnp.bfloat16)
    hidden_gradient = jnp.einsum(
        "odk,ak->oda", derivative_entire, contract_factor_entire, preferred_element_type=jnp.float32
    )
    grad_down_part = jnp.einsum(
        "meb,mer->br", hidden_activation, derivative_entire, preferred_element_type=jnp.float32
    )
    gate_gradient = gelu_back(hidden_gradient * up_preactivation)[0].astype(jnp.bfloat16)
    up_gradient = (hidden_gradient * activated).astype(jnp.bfloat16)
    grad_gate_part = jnp.einsum(
        "kwq,kwm->qm", second_normed_whole, gate_gradient, preferred_element_type=jnp.float32
    )
    grad_up_part = jnp.einsum(
        "kwq,kwm->qm", second_normed_whole, up_gradient, preferred_element_type=jnp.float32
    )
    second_norm_portion = jnp.einsum(
        "gpe,ze->gpz", gate_gradient, gate_weight_whole, preferred_element_type=jnp.float32
    )
    second_norm_portion = second_norm_portion + jnp.einsum(
        "gpe,ze->gpz", up_gradient, up_weight_whole, preferred_element_type=jnp.float32
    )
    norm_two_grad = lax.psum_scatter(
        second_norm_portion.astype(jnp.bfloat16), "tensor", scatter_dimension=1, tiled=True
    ).astype(jnp.float32)
    gain_two_grad = jnp.sum(norm_two_grad * middle * inv_two, axis=(0, 1))
    mid_grad = cotangent.astype(jnp.float32) + norm_backward(
        norm_two_grad, middle, inv_two, gain_two
    )
    mid_low = mid_grad.astype(jnp.bfloat16)
    backward_rows = lax.all_gather(mid_low, "tensor", axis=1, tiled=True)
    grad_out_part = jnp.einsum(
        "omi,omn->in", attention_head_rows, backward_rows, preferred_element_type=jnp.float32
    )
    head_grad = jnp.einsum(
        "tcm,em->tce", backward_rows, output_matrix, preferred_element_type=jnp.float32
    ).astype(jnp.bfloat16)
    head_grad_blocks = head_grad.reshape(
        seq_count * block_count, block_rows, groups_here, per_group, HEAD_DIM
    )

    def backward_block(kv_total, inputs):
        block_index, out_grad_blk, log_sum_blk = inputs
        query_blk, kv_blk, scores, seq_pos, key_start = block_parts(block_index)
        attn_probs = jnp.exp(scores - log_sum_blk[..., None])
        prob_grad = jnp.einsum(
            "qgpd,kd->gpqk", out_grad_blk, kv_blk[:, HEAD_DIM:], preferred_element_type=jnp.float32
        )
        inner_sum = jnp.sum(attn_probs * prob_grad, axis=-1, keepdims=True)
        score_grad = (attn_probs * (prob_grad - inner_sum)).astype(jnp.bfloat16)
        query_piece = (
            jnp.einsum(
                "gpqk,kd->qgpd",
                score_grad,
                kv_blk[:, :HEAD_DIM],
                preferred_element_type=jnp.float32,
            )
            * score_scale
        )
        key_piece = (
            jnp.einsum("gpqk,qgpd->gkd", score_grad, query_blk, preferred_element_type=jnp.float32)
            * score_scale
        )
        value_piece = jnp.einsum(
            "gpqk,qgpd->gkd",
            attn_probs.astype(jnp.bfloat16),
            out_grad_blk,
            preferred_element_type=jnp.float32,
        )
        both_piece = jnp.concatenate([key_piece, value_piece], axis=-1)
        current = lax.dynamic_slice(
            kv_total,
            (jnp.int32(0), seq_pos, key_start, jnp.int32(0)),
            (groups_here, 1, key_rows, 2 * HEAD_DIM),
        )
        kv_total = lax.dynamic_update_slice(
            kv_total,
            current + both_piece[:, None],
            (jnp.int32(0), seq_pos, key_start, jnp.int32(0)),
        )
        return (kv_total, query_piece.reshape(block_rows, heads_here * HEAD_DIM))

    kv_start = jnp.zeros((groups_here, seq_count, 2 * shard_len, 2 * HEAD_DIM), jnp.float32)
    kv_total, query_blocks = lax.scan(
        backward_block, kv_start, (tile_numbers, head_grad_blocks, log_sums)
    )
    query_gradient = query_blocks.reshape(seq_count, rows_here, heads_here * HEAD_DIM).astype(
        jnp.bfloat16
    )
    later_grad = from_behind(kv_total[:, :, :shard_len].astype(jnp.bfloat16), "context", -1).astype(
        jnp.float32
    )
    kv_sum = kv_total[:, :, shard_len:] + later_grad
    keyvalue_gradient = kv_sum.astype(jnp.bfloat16)
    grad_query_part = jnp.einsum(
        "wgh,wgi->hi", attention_rows, query_gradient, preferred_element_type=jnp.float32
    )
    grad_keyval_part = jnp.einsum(
        "zoy,bzoh->yh", attention_rows, keyvalue_gradient, preferred_element_type=jnp.float32
    )
    norm_one_part = jnp.einsum(
        "efz,wz->efw", query_gradient, query_matrix, preferred_element_type=jnp.float32
    )
    norm_one_part = norm_one_part + jnp.einsum(
        "qxpa,ea->xpe", keyvalue_gradient, keyvalue_weight_whole, preferred_element_type=jnp.float32
    )
    norm_one_grad = lax.psum_scatter(
        norm_one_part.astype(jnp.bfloat16), "tensor", scatter_dimension=1, tiled=True
    ).astype(jnp.float32)
    gain_one_grad = jnp.sum(norm_one_grad * input_rows * inv_one, axis=(0, 1))
    input_grad = mid_grad + norm_backward(norm_one_grad, input_rows, inv_one, gain_one)
    grad_query, grad_out, grad_gate, grad_up, grad_down = (
        lax.psum_scatter(grad_query_part, ("fsdp", "context"), scatter_dimension=0, tiled=True),
        lax.psum_scatter(grad_out_part, ("fsdp", "context"), scatter_dimension=1, tiled=True),
        lax.psum_scatter(grad_gate_part, ("fsdp", "context"), scatter_dimension=0, tiled=True),
        lax.psum_scatter(grad_up_part, ("fsdp", "context"), scatter_dimension=0, tiled=True),
        lax.psum_scatter(grad_down_part, ("fsdp", "context"), scatter_dimension=1, tiled=True),
    )
    gains_part = jnp.stack([gain_one_grad, gain_two_grad])
    grad_keyval, grad_gains = (
        lax.psum_scatter(
            grad_keyval_part, ("fsdp", "context", "tensor"), scatter_dimension=0, tiled=True
        ),
        lax.psum_scatter(
            gains_part, ("fsdp", "context", "tensor"), scatter_dimension=1, tiled=True
        ),
    )
    return (
        output,
        input_grad,
        grad_query,
        grad_keyval,
        grad_out,
        grad_gate,
        grad_up,
        grad_down,
        grad_gains,
    )


def solution(mesh):
    placed = (
        P("fsdp", ("context", "tensor"), None),
        P("fsdp", ("context", "tensor"), None),
        P("fsdp", None),
        P(("fsdp", "context"), "tensor"),
        P(("fsdp", "context", "tensor"), None),
        P("tensor", ("fsdp", "context")),
        P(("fsdp", "context"), "tensor"),
        P(("fsdp", "context"), "tensor"),
        P("tensor", ("fsdp", "context")),
        P(None, ("fsdp", "context", "tensor")),
    )
    return jax.shard_map(
        local,
        mesh=mesh,
        in_specs=placed,
        out_specs=(
            P("fsdp", ("context", "tensor"), None),
            P("fsdp", ("context", "tensor"), None),
            P(("fsdp", "context"), "tensor"),
            P(("fsdp", "context", "tensor"), None),
            P("tensor", ("fsdp", "context")),
            P(("fsdp", "context"), "tensor"),
            P(("fsdp", "context"), "tensor"),
            P("tensor", ("fsdp", "context")),
            P(None, ("fsdp", "context", "tensor")),
        ),
        check_vma=False,
    )
```

profile of v0, /device:TPU:0, one launch (start us, length us, event | category | flops | bytes accessed | tf_op | source)
XLA Modules:
  0.0 1516.6 jit_solution(6817057681967940535)
XLA Ops:
  9.2 43.2 %all-gather = bf16[32,48,2]{1,2,0:T(2,128)(2,1)S(1)} all-gather(bf16[1,48,2]{1,2,0:T(2,128)(2,1)} %bitcast.291), channel_id=1, replica_groups=mesh['fsdp'=4,'context'=2,'tensor'=4] {'fsdp','context','tensor'}, dimensions={0}, use_global_device_ids=true | all-gather | bytes 6336 | tf_op jit(solution)/shard_map/all_gather | solution.py:55
  56.4 39.2 %all_gather.35 = bf16[1536,256]{1,0:T(8,128)(2,1)S(1)} all-gather(bf16[48,256]{1,0:T(8,128)(2,1)S(1)} %copy-done.21), channel_id=1, replica_groups=mesh['fsdp'=4,'context'=2,'tensor'=4] {'fsdp','context','tensor'}, dimensions={0}, use_global_device_ids=true | all-gather | bytes 811008 | tf_op jit(solution)/shard_map/all_gather | solution.py:54
  95.6 3.2 fusion.96
  100.9 26.7 %all-gather.13.cloned.1.call-done = bf16[1536,384]{1,0:T(8,128)(2,1)} async-done(((bf16[192,384]{1,0:T(8,128)(2,1)}), bf16[1536,384]{1,0:T(8,128)(2,1)}) %all-gather.13.cloned.1.call-update) | async-done | bytes 1179664 | tf_op jit(solution)/shard_map/all_gather | solution.py:47
  127.6 4.0 fusion.90
  133.9 24.5 %while.34 = (s32[]{:T(128)}, bf16[2,512,384]{2,1,0:T(8,128)(2,1)S(1)}, f32[2,1,3,512]{3,2,1,0:T(4,128)S(1)}, s32[2]{0:T(128)S(1)}, bf16[1,2048,256]{2,1,0:T(8,12...) while((s32[]{:T(128)}, ...), condition=%wide.region_4.5_spmd, body=%wide.region_1.4_spmd.sunk | while | flops 1240400896 | bytes 37067168 | solution.py:131
  155.0 3.1 fusion.156
  158.4 11.3 all-gather.15.cloned.1.call-done
  169.7 5.8 convolution_bitcast_fusion.1
  176.3 56.4 %reduce-scatter.14.cloned.1.call-done = f32[1,256,1536]{2,1,0:T(8,128)} async-done(((f32[1,1024,1536]{2,1,0:T(8,128)}), f32[1,256,1536]{2,1,0:T(8,128)}) %reduce-scatter.14.cloned.1.call-update) | async-done | bytes 1572880 | tf_op jit(solution)/shard_map/reduce_scatter | solution.py:136
  238.0 62.2 %all-gather.21.cloned.1.call-done = bf16[1536,1152]{1,0:T(8,128)(2,1)} async-done(((bf16[192,1152]{1,0:T(8,128)(2,1)}), bf16[1536,1152]{1,0:T(8,128)(2,1)}) %all-gather.21.cloned.1.call-update) | async-done | bytes 3538960 | tf_op jit(solution)/shard_map/all_gather | solution.py:50
  300.2 29.1 %all-gather.17.cloned.1.call-done = bf16[1,1024,1536]{2,1,0:T(8,128)(2,1)} async-done(((bf16[1,256,1536]{2,1,0:T(8,128)(2,1)}), bf16[1,1024,1536]{2,1,0:T(8,128)(2,1)}) %all-gather.17.cloned.1.call-update) | async-done | bytes 3145744 | tf_op jit(solution)/shard_map/all_gather | solution.py:141
  329.4 9.3 fusion.55
  338.7 58.3 %all-gather.19.cloned.1.call-done = bf16[1536,1152]{1,0:T(8,128)(2,1)} async-done(((bf16[192,1152]{1,0:T(8,128)(2,1)}), bf16[1536,1152]{1,0:T(8,128)(2,1)}) %all-gather.19.cloned.1.call-update) | async-done | bytes 3538960 | tf_op jit(solution)/shard_map/all_gather | solution.py:49
  397.0 9.3 fusion.57
  406.3 19.4 %all-gather.25.cloned.1.call-done = bf16[1,1024,1536]{2,1,0:T(8,128)(2,1)} async-done(((bf16[1,256,1536]{2,1,0:T(8,128)(2,1)}), bf16[1,1024,1536]{2,1,0:T(8,128)(2,1)}) %all-gather.25.cloned.1.call-update) | async-done | bytes 3145744 | tf_op jit(solution)/shard_map/all_gather | solution.py:142
  425.7 67.6 %all-gather.23.cloned.1.call-done = bf16[1152,1536]{0,1:T(8,128)(2,1)} async-done(((bf16[1152,192]{0,1:T(8,128)(2,1)}), bf16[1152,1536]{0,1:T(8,128)(2,1)}) %all-gather.23.cloned.1.call-update) | async-done | bytes 3538960 | tf_op jit(solution)/shard_map/all_gather | solution.py:51
  493.3 13.2 multiply_convert_fusion
  506.6 4.3 fusion.105
  510.9 5.7 fusion.41
  516.6 36.6 %reduce-scatter.18.cloned.1.call-done = bf16[1,256,1536]{2,1,0:T(8,128)(2,1)} async-done(((bf16[1,1024,1536]{2,1,0:T(8,128)(2,1)}), bf16[1,256,1536]{2,1,0:T(8,128)(2,1)}) %reduce-scatter.18.cloned.1.call-update) | async-done | bytes 786448 | tf_op jit(solution)/shard_map/reduce_scatter | solution.py:179
  558.0 28.6 %all-gather.27.cloned.1.call-done = bf16[1,1024,1536]{2,1,0:T(8,128)(2,1)} async-done(((bf16[1,256,1536]{2,1,0:T(8,128)(2,1)}), bf16[1,1024,1536]{2,1,0:T(8,128)(2,1)}) %all-gather.27.cloned.1.call-update) | async-done | bytes 3145744 | tf_op jit(solution)/shard_map/all_gather | solution.py:187
  586.6 4.0 fusion.87
  593.6 72.8 %while.35 = (s32[]{:T(128)}, f32[1,1,2048,256]{2,3,1,0:T(8,128)}, bf16[2,512,384]{2,1,0:T(8,128)(2,1)}, s32[2]{0:T(128)S(1)}, s32[1,2048]{1,0:T(1,128)S(1)}, /*i...) while((s32[]{:T(128)}, f32[1,1,2048,256]{2,3,1,0:T(8,128)}, ...), condition=%wide.region_12.13_spmd, body=%wide.region_10.12_spmd.sunk | while | flops 3046441984 | bytes 142422512 | solution.py:240
  600.6 6.3 fusion.165
  607.2 11.0 fusion.167
  618.2 5.5 fusion.166
  637.0 6.3 fusion.165
  643.6 11.0 fusion.167
  654.6 5.5 fusion.166
  669.2 3.5 fusion.106
  672.7 10.9 collective-permute-done.1
  687.3 8.6 fusion.40
  696.0 28.5 %reduce-scatter.20.cloned.1.call-done = bf16[1,256,1536]{2,1,0:T(8,128)(2,1)} async-done(((bf16[1,1024,1536]{2,1,0:T(8,128)(2,1)}), bf16[1,256,1536]{2,1,0:T(8,128)(2,1)}) %reduce-scatter.20.cloned.1.call-update) | async-done | bytes 786448 | tf_op jit(solution)/shard_map/reduce_scatter | solution.py:263
  727.4 4.2 fusion.59
  731.6 10.4 fusion.47
  743.7 9.5 fusion.51
  754.8 9.0 fusion.53
  764.9 5.1 fusion.43
  770.5 5.1 fusion.61
  777.0 3.9 fusion.71
  781.0 84.7 %reduce-scatter.34.cloned.1.call-done = f32[48,2]{1,0:T(8,128)} async-done(((f32[1536,2]{1,0:T(8,128)}), f32[48,2]{1,0:T(8,128)}) %reduce-scatter.34.cloned.1.call-update) | async-done | bytes 400
  867.0 100.4 %reduce-scatter.24.cloned.1.call-done = f32[48,256]{1,0:T(8,128)} async-done(((f32[1536,256]{1,0:T(8,128)}), f32[48,256]{1,0:T(8,128)}) %reduce-scatter.24.cloned.1.call-update) | async-done | bytes 49168 | tf_op jit(solution)/shard_map/reduce_scatter | solution.py:277
  967.5 132.1 %reduce-scatter.32.cloned.1.call-done = f32[1152,192]{0,1:T(8,128)} async-done(((f32[1152,1536]{0,1:T(8,128)}), f32[1152,192]{0,1:T(8,128)}) %reduce-scatter.32.cloned.1.call-update) | async-done | bytes 884752 | tf_op jit(solution)/shard_map/reduce_scatter | solution.py:273
  1099.6 132.6 %reduce-scatter.30.cloned.1.call-done = f32[192,1152]{1,0:T(8,128)} async-done(((f32[1536,1152]{1,0:T(8,128)}), f32[192,1152]{1,0:T(8,128)}) %reduce-scatter.30.cloned.1.call-update) | async-done | bytes 884752 | tf_op jit(solution)/shard_map/reduce_scatter | solution.py:272
  1232.2 132.2 %reduce-scatter.28.cloned.1.call-done = f32[192,1152]{1,0:T(8,128)} async-done(((f32[1536,1152]{1,0:T(8,128)}), f32[192,1152]{1,0:T(8,128)}) %reduce-scatter.28.cloned.1.call-update) | async-done | bytes 884752 | tf_op jit(solution)/shard_map/reduce_scatter | solution.py:271
  1364.4 72.5 %reduce-scatter.26.cloned.1.call-done = f32[384,192]{0,1:T(8,128)} async-done(((f32[384,1536]{0,1:T(8,128)}), f32[384,192]{0,1:T(8,128)}) %reduce-scatter.26.cloned.1.call-update) | async-done | bytes 294928 | tf_op jit(solution)/shard_map/reduce_scatter | solution.py:270
  1437.0 72.3 %reduce-scatter.22.cloned.1.call-done = f32[192,384]{1,0:T(8,128)} async-done(((f32[1536,384]{1,0:T(8,128)}), f32[192,384]{1,0:T(8,128)}) %reduce-scatter.22.cloned.1.call-update) | async-done | bytes 294928 | tf_op jit(solution)/shard_map/reduce_scatter | solution.py:269
  (210 shorter events, 81.8 us)
Async XLA Ops:
  7.2 49.2 %copy-start.21 = (bf16[48,256]{1,0:T(8,128)(2,1)S(1)}, bf16[48,256]{1,0:T(8,128)(2,1)}, u32[]{:S(2)}) copy-start(bf16[48,256]{1,0:T(8,128)(2,1)} %param.18) | copy-start | bytes 73732
  7.2 88.4 %all-gather.11.cloned.1.call-start = ((), (), s32[]{:S(2)}) async-start(), calls=%async_computation.11 | async-start | bytes 3932160 | tf_op jit(solution)/shard_map/all_gather | solution.py:63
  9.2 89.5 %copy-start.22 = (f32[256]{0:T(256)}, f32[256]{0:T(256)S(1)}, u32[]{:S(2)}) copy-start(f32[256]{0:T(256)S(1)} %get-tuple-element.494) | copy-start | bytes 3076
  52.5 502.3 %copy-start.15 = (f32[1536]{0:T(1024)}, f32[1536]{0:T(1024)S(1)}, u32[]{:S(2)}) copy-start(f32[1536]{0:T(1024)S(1)} %get-tuple-element.444) | copy-start | bytes 18436
  54.8 72.8 %all-gather.13.cloned.1.call-start = ((), (), s32[]{:S(2)}) async-start(), calls=%async_computation.12 | async-start | bytes 1327104 | tf_op jit(solution)/shard_map/all_gather | solution.py:47
  55.6 114.1 %all-gather.15.cloned.1.call-start = ((), (), s32[]{:S(2)}) async-start(), calls=%async_computation.13 | async-start | bytes 1327104 | tf_op jit(solution)/shard_map/all_gather | solution.py:48
  56.3 176.4 %reduce-scatter.14.cloned.1.call-start = ((), (), s32[]{:S(2)}) async-start(), calls=%async_computation.14 | async-start | bytes 7864320 | tf_op jit(solution)/shard_map/reduce_scatter | solution.py:136
  98.7 34.0 %collective-permute-start = (bf16[1,1024,256]{2,1,0:T(8,128)(2,1)S(1)}, bf16[1,1024,256]{2,1,0:T(8,128)(2,1)}, u32[]{:S(2)}, u32[]{:S(2)}) collective-permute-start(bf16[1,1024,256]{2,1,0:T(8,128)(2,1)S(1)} %fusion.96), channel_id=1, source_target_pairs={{0,4},{1,5},{2,6},{3,7},{8,12},{9,13},{10,14},{11,15},{16,20},{17,... | collective-permute-start | bytes 1572872 | tf_op jit(solution)/shard_map/ppermute | solution.py:16
  158.4 17.1 %copy-start.13 = (bf16[2,512,384]{2,1,0:T(8,128)(2,1)}, bf16[2,512,384]{2,1,0:T(8,128)(2,1)S(1)}, u32[]{:S(2)}) copy-start(bf16[2,512,384]{2,1,0:T(8,128)(2,1)S(1)} %get-tuple-element.395) | copy-start | bytes 2359300
  175.5 57.3 %copy-start.5 = (bf16[1,256,1536]{2,1,0:T(8,128)(2,1)S(1)}, bf16[1,256,1536]{2,1,0:T(8,128)(2,1)}, u32[]{:S(2)}) copy-start(bf16[1,256,1536]{2,1,0:T(8,128)(2,1)} %param.14) | copy-start | bytes 2359300
  175.5 124.8 %all-gather.21.cloned.1.call-start = ((), (), s32[]{:S(2)}) async-start(), calls=%async_computation.17 | async-start | bytes 3981312 | tf_op jit(solution)/shard_map/all_gather | solution.py:50
  176.1 153.3 %all-gather.17.cloned.1.call-start = ((), (), s32[]{:S(2)}) async-start(), calls=%async_computation.15 | async-start | bytes 3932160 | tf_op jit(solution)/shard_map/all_gather | solution.py:141
  234.5 320.4 %copy-start.3 = (f32[1,256,1536]{2,1,0:T(8,128)}, f32[1,256,1536]{2,1,0:T(8,128)S(1)}, u32[]{:S(2)}) copy-start(f32[1,256,1536]{2,1,0:T(8,128)S(1)} %get-tuple-element.479) | copy-start | bytes 4718596
  234.5 320.4 %copy-start.19 = (f32[256]{0:T(256)}, f32[256]{0:T(256)S(1)}, u32[]{:S(2)}) copy-start(f32[256]{0:T(256)S(1)} %get-tuple-element.496) | copy-start | bytes 3076
  234.5 320.4 %copy-start.24 = (f32[256]{0:T(256)}, f32[256]{0:T(256)S(1)}, u32[]{:S(2)}) copy-start(f32[256]{0:T(256)S(1)} %get-tuple-element.495) | copy-start | bytes 3076
  235.8 161.2 %all-gather.19.cloned.1.call-start = ((), (), s32[]{:S(2)}) async-start(), calls=%async_computation.16 | async-start | bytes 3981312 | tf_op jit(solution)/shard_map/all_gather | solution.py:49
  236.5 189.2 %all-gather.25.cloned.1.call-start = ((), (), s32[]{:S(2)}) async-start(), calls=%async_computation.20 | async-start | bytes 3932160 | tf_op jit(solution)/shard_map/all_gather | solution.py:142
  237.3 256.1 %all-gather.23.cloned.1.call-start = ((), (), s32[]{:S(2)}) async-start(), calls=%async_computation.18 | async-start | bytes 3981312 | tf_op jit(solution)/shard_map/all_gather | solution.py:51
  238.0 315.2 %reduce-scatter.18.cloned.1.call-start = ((), (), s32[]{:S(2)}) async-start(), calls=%async_computation.21 | async-start | bytes 3932160 | tf_op jit(solution)/shard_map/reduce_scatter | solution.py:179
  493.3 13.3 copy-start.31
  516.6 38.8 %copy-start.7 = (bf16[1,256,1536]{2,1,0:T(8,128)(2,1)S(1)}, bf16[1,256,1536]{2,1,0:T(8,128)(2,1)}, u32[]{:S(2)}) copy-start(bf16[1,256,1536]{2,1,0:T(8,128)(2,1)} %param.15) | copy-start | bytes 2359300
  516.6 70.0 %all-gather.27.cloned.1.call-start = ((), (), s32[]{:S(2)}) async-start(), calls=%async_computation.22 | async-start | bytes 3932160 | tf_op jit(solution)/shard_map/all_gather | solution.py:187
  557.9 166.5 %reduce-scatter.20.cloned.1.call-start = ((), (), s32[]{:S(2)}) async-start(), calls=%async_computation.23 | async-start | bytes 3932160 | tf_op jit(solution)/shard_map/reduce_scatter | solution.py:263
  600.6 6.6 copy-start
  618.2 5.5 copy-start.1
  637.0 6.6 copy-start
  654.6 5.5 copy-start.1
  667.7 16.0 %collective-permute-start.1 = (bf16[1,1,1024,256]{2,3,1,0:T(8,128)(2,1)S(1)}, bf16[1,1,1024,256]{2,3,1,0:T(8,128)(2,1)S(1)}, u32[]{:S(2)}, u32[]{:S(2)}) collective-permute-start(bf16[1,1,1024,256]{2,3,1,0:T(8,128)(2,1)S(1)} %slice.86), channel_id=1, source_target_pairs={{4,0},{5,1},{6,2},{7,3},{12,8},{13,9},{14,10},{15,11},{20,16},{21,... | collective-permute-start | bytes 1572872 | tf_op jit(solution)/shard_map/ppermute | solution.py:16
  669.2 15.2 %copy-start.2 = (f32[1,1,2048,256]{2,3,1,0:T(8,128)S(1)}, f32[1,1,2048,256]{2,3,1,0:T(8,128)}, u32[]{:S(2)}) copy-start(f32[1,1,2048,256]{2,3,1,0:T(8,128)} %get-tuple-element.398) | copy-start | bytes 6291460
  669.2 15.2 %copy-start.10 = (bf16[1536,256]{1,0:T(8,128)(2,1)S(1)}, bf16[1536,256]{1,0:T(8,128)(2,1)}, u32[]{:S(2)}) copy-start(bf16[1536,256]{1,0:T(8,128)(2,1)} %copy-done.9) | copy-start | bytes 2359300
  687.2 88.5 %reduce-scatter.16.cloned.1.call-start = ((), (), s32[]{:S(2)}) async-start(), calls=%async_computation.19 | async-start | bytes 3932160 | tf_op jit(solution)/shard_map/reduce_scatter | solution.py:155
  695.9 28.5 %copy-start.6 = (bf16[1,256,1536]{2,1,0:T(8,128)(2,1)S(1)}, bf16[1,256,1536]{2,1,0:T(8,128)(2,1)}, u32[]{:S(2)}) copy-start(bf16[1,256,1536]{2,1,0:T(8,128)(2,1)} %param.14) | copy-start | bytes 2359300
  695.9 28.5 %copy-start.18 = (f32[1536]{0:T(1024)S(1)}, f32[1536]{0:T(1024)}, u32[]{:S(2)}) copy-start(f32[1536]{0:T(1024)} %copy-done.17) | copy-start | bytes 18436
  695.9 28.5 %copy-start.23 = (f32[256]{0:T(256)S(1)}, f32[256]{0:T(256)}, u32[]{:S(2)}) copy-start(f32[256]{0:T(256)} %copy-done.22) | copy-start | bytes 3076
  695.9 169.7 %reduce-scatter.34.cloned.1.call-start = ((), (), s32[]{:S(2)}) async-start(), calls=%async_computation.30 | async-start | bytes 811008
  727.3 240.1 %reduce-scatter.24.cloned.1.call-start = ((), (), s32[]{:S(2)}) async-start(), calls=%async_computation.25 | async-start | bytes 1622016 | tf_op jit(solution)/shard_map/reduce_scatter | solution.py:277
  731.6 368.0 %reduce-scatter.32.cloned.1.call-start = ((), (), s32[]{:S(2)}) async-start(), calls=%async_computation.29 | async-start | bytes 7962624 | tf_op jit(solution)/shard_map/reduce_scatter | solution.py:273
  742.0 490.2 %reduce-scatter.30.cloned.1.call-start = ((), (), s32[]{:S(2)}) async-start(), calls=%async_computation.28 | async-start | bytes 7962624 | tf_op jit(solution)/shard_map/reduce_scatter | solution.py:272
  753.1 611.3 %reduce-scatter.28.cloned.1.call-start = ((), (), s32[]{:S(2)}) async-start(), calls=%async_computation.27 | async-start | bytes 7962624 | tf_op jit(solution)/shard_map/reduce_scatter | solution.py:271
  763.8 6.7 copy-start.12
  763.8 673.1 %reduce-scatter.26.cloned.1.call-start = ((), (), s32[]{:S(2)}) async-start(), calls=%async_computation.26 | async-start | bytes 2654208 | tf_op jit(solution)/shard_map/reduce_scatter | solution.py:270
  770.1 5.6 copy-start.8
  770.1 5.6 copy-start.16
  770.1 5.6 copy-start.20
  770.1 5.6 copy-start.25
  770.1 5.6 copy-start.27
  770.1 5.6 copy-start.29
  770.1 739.2 %reduce-scatter.22.cloned.1.call-start = ((), (), s32[]{:S(2)}) async-start(), calls=%async_computation.24 | async-start | bytes 2654208 | tf_op jit(solution)/shard_map/reduce_scatter | solution.py:269
  (12 other events, 32.5 us)
Sparse Core Ops, SparseCore 0:
  54.9 29.6 all-gather.10
  86.8 40.7 all-gather.12
  129.8 39.8 all-gather.14
  175.6 57.1 reduce-scatter.13
  235.0 65.1 all-gather.20
  302.3 27.0 all-gather.16
  331.8 65.1 all-gather.18
  398.6 27.0 all-gather.24
  428.1 65.1 all-gather.22
  516.7 36.4 reduce-scatter.17
  558.1 28.5 all-gather.26
  687.4 37.0 reduce-scatter.19
  727.1 37.9 reduce-scatter.15
  770.1 95.5 reduce-scatter.33
  871.3 96.0 reduce-scatter.23
  971.6 127.9 reduce-scatter.31
  1104.1 128.0 reduce-scatter.29
  1236.3 128.0 reduce-scatter.27
  1368.9 67.9 reduce-scatter.25
  1441.3 67.9 reduce-scatter.21
where the time goes:
time: 1530 us; the launch traced here: 1520 us
  waiting for transfers between devices  1170 us (76%)
  matrix products  160 us (10%)
  blocking collectives  82.4 us (5%)
  other arithmetic  54.2 us (4%)
  local copies, waits for them, and re-layouts  24.8 us (2%)
  between operations  15.3 us (1%)
    reduce_scatter x1, waiting for transfers between devices, local(): lax.psum_scatter(grad_up_part, ('fsdp', 'context'), scatter_dimension=0,...  133 us
    reduce_scatter x1, waiting for transfers between devices, local(): lax.psum_scatter(grad_gate_part, ('fsdp', 'context'), scatter_dimension=0...  132 us
    reduce_scatter x1, waiting for transfers between devices, local(): lax.psum_scatter(grad_down_part, ('fsdp', 'context'), scatter_dimension=1...  132 us
    reduce_scatter x1, waiting for transfers between devices, local(): lax.psum_scatter(grad_keyval_part, ('fsdp', 'context', 'tensor'), scatter...  100 us
    unnamed x21, waiting for transfers between devices  88.9 us
    reduce_scatter x1, waiting for transfers between devices, local(): lax.psum_scatter(grad_out_part, ('fsdp', 'context'), scatter_dimension=1,...  72.5 us
    reduce_scatter x1, waiting for transfers between devices, local(): lax.psum_scatter(grad_query_part, ('fsdp', 'context'), scatter_dimension=...  72.3 us
    all_gather x1, waiting for transfers between devices, local(): lax.all_gather(contract_factor, ('fsdp', 'context'), axis=1, tiled=True)  67.6 us
  transfers between devices with their start and end apart: 22, of which 19 were waited for; matrix products, arithmetic and copies ran while one was open for 8% of the time, Pallas kernels for 0%

commit v1 on v0

v1 whole, which is shorter than its diff:
```python
import functools

import jax
import jax.numpy as jnp
from jax import lax
from jax.experimental import pallas as pl
from jax.experimental.pallas import tpu as pltpu
from jax.sharding import PartitionSpec as P

HEAD_DIM = 128
WINDOW = 1024
EPSILON = 1e-06
LOG2E = 1.4426950408889634
SCALE = HEAD_DIM**-0.5
BF = jnp.bfloat16
F32 = jnp.float32


def swap(value, axis, k):
    count = lax.axis_size(axis)
    return lax.ppermute(value, axis, [(i, i ^ k) for i in range(count)])


def shift(value, axis, steps):
    count = lax.axis_size(axis)
    leading, last = max(0, -steps), min(count, count - steps)
    return lax.ppermute(value, axis, [(i, i + steps) for i in range(leading, last)])


def bits_of(count):
    return [1 << b for b in range(count.bit_length() - 1)]


def tensor_order(count):
    order = [0]
    for bit in reversed(bits_of(count)):
        order = order + [k ^ bit for k in order]
    return order


def gather_tensor(value):
    pieces = [value]
    for bit in reversed(bits_of(lax.axis_size("tensor"))):
        pieces = pieces + [swap(p, "tensor", bit) for p in pieces]
    return jnp.concatenate(pieces, axis=0)


def reduce_tensor(make, rows):
    half = rows // 2
    away = make(half, rows).astype(BF)
    bits = bits_of(lax.axis_size("tensor"))
    back = swap(away, "tensor", bits[0])
    total = make(0, half) + back.astype(F32)
    for bit in bits[1:]:
        half //= 2
        back = swap(total[half:].astype(BF), "tensor", bit)
        total = total[:half] + back.astype(F32)
    return total


def gather_weight(shard):
    nf, nc = lax.axis_size("fsdp"), lax.axis_size("context")
    f, c = lax.axis_index("fsdp"), lax.axis_index("context")
    along = [shard] + [swap(shard, "fsdp", k) for k in range(1, nf)]
    whole = jnp.zeros((nf * nc,) + shard.shape, shard.dtype)
    for kf in range(nf):
        for kc in range(nc):
            piece = along[kf] if kc == 0 else swap(along[kf], "context", kc)
            whole = lax.dynamic_update_index_in_dim(whole, piece, (f ^ kf) * nc + (c ^ kc), 0)
    return whole.reshape(nf * nc * shard.shape[0], shard.shape[1])


def scatter_grad(part):
    nf, nc = lax.axis_size("fsdp"), lax.axis_size("context")
    f, c = lax.axis_index("fsdp"), lax.axis_index("context")
    slabs = part.reshape(nf, nc, part.shape[0] // (nf * nc), part.shape[1])
    total = lax.dynamic_index_in_dim(slabs, c, 1, False).astype(F32)
    for k in range(1, nc):
        total = total + swap(lax.dynamic_index_in_dim(slabs, c ^ k, 1, False), "context", k).astype(F32)
    own = lax.dynamic_index_in_dim(total, f, 0, False)
    for k in range(1, nf):
        sent = lax.dynamic_index_in_dim(total, f ^ k, 0, False).astype(BF)
        own = own + swap(sent, "fsdp", k).astype(F32)
    return own


def dot_nt(a, b):
    return lax.dot_general(a, b, (((1,), (1,)), ((), ())), preferred_element_type=F32)


def dot_nn(a, b):
    return lax.dot_general(a, b, (((1,), (0,)), ((), ())), preferred_element_type=F32)


def in_order(blocks_ref, prev_ref, own_ref, both, count, rows):
    for r in range(count):
        at = blocks_ref[r] * rows
        both[pl.ds(at, rows), :] = prev_ref[r * rows : (r + 1) * rows, :]
        both[pl.ds(at + count * rows, rows), :] = own_ref[r * rows : (r + 1) * rows, :]


def fill_bias(a, rows, count, qseg_ref, kseg_ref, bias, tri):
    qs = qseg_ref[...]
    wide = rows // 128

    def seg(i):
        s = kseg_ref[pl.ds((a + i) * rows, rows), :]
        return jnp.concatenate([s] * wide, axis=1) == qs

    first = (tri & seg(count)) | (jnp.logical_not(tri) & seg(0))
    bias[0] = jnp.where(first, 0.0, -1e30).astype(F32)
    for i in range(1, count):
        bias[i] = jnp.where(seg(i), 0.0, -1e30).astype(F32)


def attend_forward(blocks_ref, q_ref, prev_ref, own_ref, qseg_ref, kseg_ref, out_ref, lse_ref, both, vt, bias):
    count, rows, heads = bias.shape[0], q_ref.shape[0], q_ref.shape[1] // HEAD_DIM
    r = pl.program_id(0)
    a = blocks_ref[r]

    @pl.when(r == 0)
    def _():
        in_order(blocks_ref, prev_ref, own_ref, both, count, rows)
        for i in range(2 * count):
            vt[:, i * rows : (i + 1) * rows] = both[i * rows : (i + 1) * rows, HEAD_DIM:].T

    tri = lax.broadcasted_iota(jnp.int32, (rows, rows), 0) <= lax.broadcasted_iota(jnp.int32, (rows, rows), 1)
    fill_bias(a, rows, count, qseg_ref, kseg_ref, bias, tri)
    starts = [pl.multiple_of((a + i) * rows, rows) for i in range(count + 1)]
    for h in range(heads):
        q = q_ref[:, h * HEAD_DIM : (h + 1) * HEAD_DIM]
        s = [dot_nt(both[pl.ds(st, rows), :HEAD_DIM], q) for st in starts]
        s = [jnp.where(tri, s[count], s[0])] + s[1:count]
        s = [x * (SCALE * LOG2E) + bias[i] for i, x in enumerate(s)]
        top = functools.reduce(jnp.maximum, s)
        top = jnp.max(top, axis=0, keepdims=True)
        p = [jnp.exp2(x - top) for x in s]
        total = jnp.sum(functools.reduce(jnp.add, p), axis=0, keepdims=True)
        low = [x.astype(BF) for x in p]
        zero = jnp.zeros_like(low[0])
        low = [jnp.where(tri, zero, low[0])] + low[1:] + [jnp.where(tri, low[0], zero)]
        acc = None
        for i in range(count + 1):
            d = dot_nn(vt[:, pl.ds(starts[i], rows)], low[i])
            acc = d if acc is None else acc + d
        out_ref[:, h * HEAD_DIM : (h + 1) * HEAD_DIM] = (acc / total).T.astype(BF)
        lse_ref[h : h + 1, :] = top + jnp.log2(total)


def attend_backward(
    blocks_ref, q_ref, prev_ref, own_ref, qseg_ref, kseg_ref, dout_ref, lse_ref, dq_ref, dprev_ref, down_ref, both, kt, bias, dkv
):
    count, rows, heads = bias.shape[0], q_ref.shape[0], q_ref.shape[1] // HEAD_DIM
    r = pl.program_id(0)
    a = blocks_ref[r]

    @pl.when(r == 0)
    def _():
        in_order(blocks_ref, prev_ref, own_ref, both, count, rows)
        for i in range(2 * count):
            kt[:, i * rows : (i + 1) * rows] = both[i * rows : (i + 1) * rows, :HEAD_DIM].T
        dkv[...] = jnp.zeros_like(dkv)

    tri = lax.broadcasted_iota(jnp.int32, (rows, rows), 0) <= lax.broadcasted_iota(jnp.int32, (rows, rows), 1)
    fill_bias(a, rows, count, qseg_ref, kseg_ref, bias, tri)
    starts = [pl.multiple_of((a + i) * rows, rows) for i in range(count + 1)]
    for h in range(heads):
        cols = slice(h * HEAD_DIM, (h + 1) * HEAD_DIM)
        q, dout = q_ref[:, cols], dout_ref[:, cols]
        lse = lse_ref[h : h + 1, :]
        s = [dot_nt(both[pl.ds(st, rows), :HEAD_DIM], q) for st in starts]
        dp = [dot_nt(both[pl.ds(st, rows), HEAD_DIM:], dout) for st in starts]
        s = [jnp.where(tri, s[count], s[0])] + s[1:count]
        dp = [jnp.where(tri, dp[count], dp[0])] + dp[1:count]
        p = [jnp.exp2(x * (SCALE * LOG2E) + bias[i] - lse) for i, x in enumerate(s)]
        inner = functools.reduce(jnp.add, [x * y for x, y in zip(p, dp)])
        inner = jnp.sum(inner, axis=0, keepdims=True)
        ds = [(x * (y - inner)).astype(BF) for x, y in zip(p, dp)]
        low = [x.astype(BF) for x in p]
        zero = jnp.zeros_like(low[0])
        low = [jnp.where(tri, zero, low[0])] + low[1:] + [jnp.where(tri, low[0], zero)]
        ds = [jnp.where(tri, zero, ds[0])] + ds[1:] + [jnp.where(tri, ds[0], zero)]
        acc = None
        for i in range(count + 1):
            d = dot_nn(kt[:, pl.ds(starts[i], rows)], ds[i])
            acc = d if acc is None else acc + d
            dkv[pl.ds(starts[i], rows), :HEAD_DIM] += dot_nn(ds[i], q)
            dkv[pl.ds(starts[i], rows), HEAD_DIM:] += dot_nn(low[i], dout)
        dq_ref[:, cols] = (acc * SCALE).T.astype(BF)

    @pl.when(r == count - 1)
    def _():
        for j in range(count):
            at = blocks_ref[j] * rows
            for ref, base in ((dprev_ref, 0), (down_ref, count * rows)):
                blk = dkv[pl.ds(at + base, rows), :]
                ref[j * rows : (j + 1) * rows, :HEAD_DIM] = (blk[:, :HEAD_DIM] * SCALE).astype(ref.dtype)
                ref[j * rows : (j + 1) * rows, HEAD_DIM:] = blk[:, HEAD_DIM:].astype(ref.dtype)


def whole_spec(shape):
    return pl.BlockSpec(shape, lambda r, b: (0,) * len(shape))


def attention_forward(blocks, queries, prev, own, qseg, kseg, count):
    total, width = queries.shape
    rows = total // count
    heads = width // HEAD_DIM
    return pl.pallas_call(
        attend_forward,
        grid_spec=pltpu.PrefetchScalarGridSpec(
            num_scalar_prefetch=1,
            grid=(count,),
            in_specs=[
                pl.BlockSpec((rows, width), lambda r, b: (r, 0)),
                whole_spec(prev.shape),
                whole_spec(own.shape),
                pl.BlockSpec((1, rows), lambda r, b: (0, b[r])),
                whole_spec(kseg.shape),
            ],
            out_specs=[
                pl.BlockSpec((rows, width), lambda r, b: (r, 0)),
                pl.BlockSpec((heads, rows), lambda r, b: (0, r)),
            ],
            scratch_shapes=[
                pltpu.VMEM((2 * total, 2 * HEAD_DIM), BF),
                pltpu.VMEM((HEAD_DIM, 2 * total), BF),
                pltpu.VMEM((count, rows, rows), F32),
            ],
        ),
        out_shape=[jax.ShapeDtypeStruct((total, width), BF), jax.ShapeDtypeStruct((heads, total), F32)],
        compiler_params=pltpu.CompilerParams(vmem_limit_bytes=40 << 20),
        cost_estimate=pl.CostEstimate(flops=4 * total * WINDOW * width, bytes_accessed=6 << 20, transcendentals=heads * total * WINDOW),
        name="attend_forward",
    )(blocks, queries, prev, own, qseg, kseg)


def attention_backward(blocks, queries, prev, own, qseg, kseg, dout, lse, count):
    total, width = queries.shape
    rows = total // count
    heads = width // HEAD_DIM
    return pl.pallas_call(
        attend_backward,
        grid_spec=pltpu.PrefetchScalarGridSpec(
            num_scalar_prefetch=1,
            grid=(count,),
            in_specs=[
                pl.BlockSpec((rows, width), lambda r, b: (r, 0)),
                whole_spec(prev.shape),
                whole_spec(own.shape),
                pl.BlockSpec((1, rows), lambda r, b: (0, b[r])),
                whole_spec(kseg.shape),
                pl.BlockSpec((rows, width), lambda r, b: (r, 0)),
                pl.BlockSpec((heads, rows), lambda r, b: (0, r)),
            ],
            out_specs=[
                pl.BlockSpec((rows, width), lambda r, b: (r, 0)),
                whole_spec(prev.shape),
                whole_spec(own.shape),
            ],
            scratch_shapes=[
                pltpu.VMEM((2 * total, 2 * HEAD_DIM), BF),
                pltpu.VMEM((HEAD_DIM, 2 * total), BF),
                pltpu.VMEM((count, rows, rows), F32),
                pltpu.VMEM((2 * total, 2 * HEAD_DIM), F32),
            ],
        ),
        out_shape=[
            jax.ShapeDtypeStruct((total, width), BF),
            jax.ShapeDtypeStruct(prev.shape, BF),
            jax.ShapeDtypeStruct(own.shape, F32),
        ],
        compiler_params=pltpu.CompilerParams(vmem_limit_bytes=40 << 20),
        cost_estimate=pl.CostEstimate(flops=10 * total * WINDOW * width, bytes_accessed=10 << 20, transcendentals=heads * total * WINDOW),
        name="attend_backward",
    )(blocks, queries, prev, own, qseg, kseg, dout, lse)


def rms_inverse(values):
    return lax.rsqrt(jnp.mean(values * values, axis=-1, keepdims=True) + EPSILON)


def norm_backward(grad_normed, values, inv_rms, gain_row):
    scaled = grad_normed * gain_row
    inner_sum = jnp.mean(scaled * values, axis=-1, keepdims=True)
    return inv_rms * scaled - values * (inv_rms * inv_rms * inv_rms) * inner_sum


def mm(a, b):
    return dot_nn(a, b)


def mm_tn(a, b):
    return lax.dot_general(a, b, (((0,), (0,)), ((), ())), preferred_element_type=F32)


def local(tokens, cotangent, segment_ids, w_query, w_keyval, w_out, w_gate, w_up, w_down, norm_gains):
    nt = lax.axis_size("tensor")
    t, c = lax.axis_index("tensor"), lax.axis_index("context")
    tokens, cotangent = tokens[0], cotangent[0]
    own_rows, width = tokens.shape
    rows = own_rows * nt
    if rows != WINDOW:
        raise ValueError("shard length")
    order = tensor_order(nt)
    blocks = jnp.array(order, jnp.int32) ^ t

    token_rows = gather_tensor(tokens)
    cot_rows = gather_tensor(cotangent)

    part = w_keyval.shape[0]
    kv_cols = w_keyval.shape[1]
    small = jnp.concatenate([w_keyval, norm_gains.T, jnp.zeros((part, 126), BF)], axis=1)
    pieces = gather_tensor(small[None])
    small = jnp.zeros_like(pieces)
    for i in range(nt):
        small = lax.dynamic_update_index_in_dim(small, pieces[i], blocks[i], 0)
    small = small.reshape(nt * part, small.shape[2])
    first = gather_weight(jnp.concatenate([w_query, small], axis=1))
    qcols = w_query.shape[1]
    wq, wkv = first[:, :qcols], first[:, qcols : qcols + kv_cols]
    gains = first[:, qcols + kv_cols : qcols + kv_cols + 2].T.astype(F32)
    gain_one, gain_two = gains[0:1], gains[1:2]
    wo_t = gather_weight(w_out.T)
    wg = gather_weight(w_gate)
    wu = gather_weight(w_up)
    wd_t = gather_weight(w_down.T)

    ids = segment_ids[0]
    own_seg = lax.dynamic_slice_in_dim(ids, c * rows, rows, 0)
    prev_seg = lax.dynamic_slice_in_dim(ids, jnp.maximum(c - 1, 0) * rows, rows, 0)
    prev_seg = jnp.where(c > 0, prev_seg, -1)
    qseg = own_seg[None, :]
    kseg = jnp.broadcast_to(jnp.concatenate([prev_seg, own_seg])[:, None], (2 * rows, 128))

    xin = token_rows.astype(F32)
    inv_one_rows = rms_inverse(xin)
    normed_one = (xin * inv_one_rows * gain_one).astype(BF)
    keyvals = mm(normed_one, wkv).astype(BF)
    earlier = shift(keyvals, "context", 1)
    queries = mm(normed_one, wq).astype(BF)
    heads_out, lse = attention_forward(blocks, queries, earlier, keyvals, qseg, kseg, nt)
    branch = reduce_tensor(lambda i, j: dot_nt(heads_out[i:j], wo_t), rows)
    own_in = tokens.astype(F32)
    middle = own_in + branch
    inv_two = rms_inverse(middle)
    normed_two = (middle * inv_two * gain_two).astype(BF)
    second_rows = gather_tensor(normed_two)

    gate_pre = mm(second_rows, wg)
    up_pre = mm(second_rows, wu)
    activated, gelu_back = jax.vjp(lambda g: jax.nn.gelu(g, approximate=True), gate_pre)
    hidden = (activated * up_pre).astype(BF)
    grad_down = scatter_grad(mm_tn(cot_rows, hidden).astype(BF)).T
    d_hidden = mm(cot_rows, wd_t)
    d_gate = gelu_back(d_hidden * up_pre)[0].astype(BF)
    d_up = (d_hidden * activated).astype(BF)
    grad_gate = scatter_grad(mm_tn(second_rows, d_gate).astype(BF))
    grad_up = scatter_grad(mm_tn(second_rows, d_up).astype(BF))
    d_two = reduce_tensor(lambda i, j: dot_nt(d_gate[i:j], wg) + dot_nt(d_up[i:j], wu), rows)
    ffn = reduce_tensor(lambda i, j: dot_nt(hidden[i:j], wd_t), rows)
    output = (middle + ffn).astype(BF)

    gain_two_part = jnp.sum(d_two * middle * inv_two, axis=0, keepdims=True)
    d_middle = cotangent.astype(F32) + norm_backward(d_two, middle, inv_two, gain_two)
    back_rows = gather_tensor(d_middle.astype(BF))
    grad_out = scatter_grad(mm_tn(back_rows, heads_out).astype(BF)).T
    d_head = mm(back_rows, wo_t).astype(BF)
    dq, dprev, dkv = attention_backward(blocks, queries, earlier, keyvals, qseg, kseg, d_head, lse, nt)
    dkv = (dkv + shift(dprev, "context", -1).astype(F32)).astype(BF)
    grad_query = scatter_grad(mm_tn(normed_one, dq).astype(BF))
    d_one = reduce_tensor(lambda i, j: dot_nt(dq[i:j], wq) + dot_nt(dkv[i:j], wkv), rows)
    inv_one = rms_inverse(own_in)
    gain_one_part = jnp.sum(d_one * own_in * inv_one, axis=0, keepdims=True)
    input_grad = d_middle + norm_backward(d_one, own_in, inv_one, gain_one)

    gains_part = jnp.concatenate([gain_one_part, gain_two_part, jnp.zeros((126, width), F32)], axis=0).T
    small_part = jnp.concatenate([mm_tn(normed_one, dkv), gains_part], axis=1).astype(BF)
    mine = scatter_grad(small_part).reshape(nt, part, kv_cols + 128)
    mine = jnp.stack([lax.dynamic_index_in_dim(mine, blocks[i], 0, False) for i in range(nt)])
    mine = reduce_tensor(lambda i, j: mine[i:j], nt)[0]
    grad_keyval = mine[:, :kv_cols]
    grad_gains = mine[:, kv_cols : kv_cols + 2].T
    return (output[None], input_grad[None], grad_query, grad_keyval, grad_out, grad_gate, grad_up, grad_down, grad_gains)


def solution(mesh):
    rows = P("fsdp", ("context", "tensor"), None)
    column = P(("fsdp", "context"), "tensor")
    row = P("tensor", ("fsdp", "context"))
    small = P(("fsdp", "context", "tensor"), None)
    gains = P(None, ("fsdp", "context", "tensor"))
    return jax.shard_map(
        local,
        mesh=mesh,
        in_specs=(rows, rows, P("fsdp", None), column, small, row, column, column, row, gains),
        out_specs=(rows, rows, column, small, row, column, column, row, gains),
        check_vma=False,
    )
```

time: 1530 us -> 623 us (0.41)
  waiting for transfers between devices: 1170 us -> 287 us
  starting transfers between devices: 5.16 us -> 146 us
  blocking collectives: 82.4 us -> 0 us
  matrix products: 160 us -> 91.6 us
  other arithmetic: 54.2 us -> 23.2 us
  Pallas kernels: 0 us -> 25.3 us
    reduce_scatter x10 -> x0, waiting for transfers between devices: 764 us -> none  [the longest x1 133 us: local(): lax.psum_scatter(grad_up_part, ('fsdp', 'context'), scatter_dimension=0,...]
    all_gather x9 -> x0, waiting for transfers between devices: 303 us -> none  [the longest x1 67.6 us: local(): lax.all_gather(contract_factor, ('fsdp', 'context'), axis=1, tiled=True)]
    ppermute x2 -> x86, waiting for transfers between devices: 10.9 us -> 287 us  [the longest x84 280 us: swap(): return lax.ppermute(value, axis, [(i, i ^ k) for i in range(count)])]
    ppermute x2 -> x86, starting transfers between devices: 3.59 us -> 146 us  [the longest x84 141 us: swap(): return lax.ppermute(value, axis, [(i, i ^ k) for i in range(count)])]
    unnamed x21 -> x0, waiting for transfers between devices: 88.9 us -> none
    all_gather x2 -> x0, blocking collectives: 82.4 us -> none  [the longest x1 43.2 us: local(): lax.all_gather(norm_gains, ('fsdp', 'context', 'tensor'), axis=1, tiled=T...]
    dot_general x32 -> x24, matrix products: 160 us -> 91.6 us  [the longest x6 37.6 us: dot_nn(): lax.dot_general(a, b, (((1,), (0,)), ((), ())), preferred_element_type=F32)]
    pallas_call x0 -> x2, Pallas kernels: none -> 25.3 us  [the longest x1 15.7 us: attention_backward(): pl.pallas_call(attend_backward, grid_spec=pltpu.PrefetchScalarGridSpec(nu...]
  transfers between devices with their start and end apart: 22 -> 86, of which waited for: 19 -> 35; matrix products, arithmetic and copies ran while one was open for 8% -> 17% of each run, Pallas kernels for 0% -> 4%
where the time goes in v1:
time: 623 us; the launch traced here: 614 us
  waiting for transfers between devices  287 us (46%)
  starting transfers between devices  146 us (23%)
  matrix products  91.6 us (15%)
  local copies, waits for them, and re-layouts  31.3 us (5%)
  Pallas kernels  25.3 us (4%)
  other arithmetic  23.2 us (4%)
  between operations  10 us (2%)
    ppermute x84, waiting for transfers between devices, swap(): return lax.ppermute(value, axis, [(i, i ^ k) for i in range(count)])  280 us
    ppermute x84, starting transfers between devices, swap(): return lax.ppermute(value, axis, [(i, i ^ k) for i in range(count)])  141 us
    dot_general x6, matrix products, dot_nn(): lax.dot_general(a, b, (((1,), (0,)), ((), ())), preferred_element_type=F32)  37.6 us
    dot_general x12, matrix products, dot_nt(): lax.dot_general(a, b, (((1,), (1,)), ((), ())), preferred_element_type=F32)  30.6 us
    dot_general x6, matrix products, mm_tn(): lax.dot_general(a, b, (((0,), (0,)), ((), ())), preferred_element_type=F32)  23.4 us
    pallas_call x1, Pallas kernels, attention_backward(): pl.pallas_call(attend_backward, grid_spec=pltpu.PrefetchScalarGridSpec(nu...  15.7 us
    dynamic_update_slice x39, local copies, waits for them, and re-layouts, gather_weight(): lax.dynamic_update_index_in_dim(whole, piece, (f ^ kf) * nc + (c ^ kc), 0)  14.1 us
  transfers between devices with their start and end apart: 86, of which 35 were waited for; matrix products, arithmetic and copies ran while one was open for 17% of the time, Pallas kernels for 4%

profile of v1, /device:TPU:0, one launch (start us, length us, event | category | flops | bytes accessed | tf_op | source)
XLA Modules:
  0.0 614.3 jit_solution(8529091370821599000)
XLA Ops:
  32.0 8.7 %collective-permute-done.17 = bf16[192,384]{1,0:T(8,128)(2,1)S(1)} collective-permute-done((bf16[192,384]{1,0:T(8,128)(2,1)}, bf16[192,384]{1,0:T(8,128)(2,1)S(1)}, u32[]{:S(2)}, u32[]{:S(2)}) %collective-permute-start.17) | collective-permute-done | bytes 147488 | tf_op jit(solution)/shard_map/ppermute | solution.py:21
  43.4 13.6 %collective-permute-done.18 = bf16[192,384]{1,0:T(8,128)(2,1)S(1)} collective-permute-done((bf16[192,384]{1,0:T(8,128)(2,1)S(1)}, bf16[192,384]{1,0:T(8,128)(2,1)S(1)}, u32[]{:S(2)}, u32[]{:S(2)}) %collective-permute-start.18) | collective-permute-done | bytes 147488 | tf_op jit(solution)/shard_map/ppermute | solution.py:21
  57.6 7.3 %collective-permute-done.20 = bf16[192,384]{1,0:T(8,128)(2,1)S(1)} collective-permute-done((bf16[192,384]{1,0:T(8,128)(2,1)S(1)}, bf16[192,384]{1,0:T(8,128)(2,1)S(1)}, u32[]{:S(2)}, u32[]{:S(2)}) %collective-permute-start.20) | collective-permute-done | bytes 147488 | tf_op jit(solution)/shard_map/ppermute | solution.py:21
  67.0 12.5 %collective-permute-done.7 = bf16[192,768]{1,0:T(8,128)(2,1)S(1)} collective-permute-done((bf16[192,768]{1,0:T(8,128)(2,1)S(1)}, bf16[192,768]{1,0:T(8,128)(2,1)S(1)}, u32[]{:S(2)}, u32[]{:S(2)}) %collective-permute-start.7) | collective-permute-done | bytes 294944 | tf_op jit(solution)/shard_map/ppermute | solution.py:21
  80.4 6.4 %collective-permute-done.34 = bf16[192,1152]{1,0:T(8,128)(2,1)S(1)} collective-permute-done((bf16[192,1152]{1,0:T(8,128)(2,1)S(1)}, bf16[192,1152]{1,0:T(8,128)(2,1)S(1)}, u32[]{:S(2)}, u32[]{:S(2)}) %collective-permute-start.34) | collective-permute-done | bytes 442400 | tf_op jit(solution)/shard_map/ppermute | solution.py:21
  91.0 9.7 %collective-permute-done.41 = bf16[192,1152]{1,0:T(8,128)(2,1)S(1)} collective-permute-done((bf16[192,1152]{1,0:T(8,128)(2,1)S(1)}, bf16[192,1152]{1,0:T(8,128)(2,1)S(1)}, u32[]{:S(2)}, u32[]{:S(2)}) %collective-permute-start.41) | collective-permute-done | bytes 442400 | tf_op jit(solution)/shard_map/ppermute | solution.py:21
  105.9 10.9 %collective-permute-done.27 = bf16[192,1152]{1,0:T(8,128)(2,1)S(1)} collective-permute-done((bf16[192,1152]{1,0:T(8,128)(2,1)S(1)}, bf16[192,1152]{1,0:T(8,128)(2,1)S(1)}, u32[]{:S(2)}, u32[]{:S(2)}) %collective-permute-start.27) | collective-permute-done | bytes 442400 | tf_op jit(solution)/shard_map/ppermute | solution.py:21
  119.0 4.9 collective-permute-done.8
  127.6 4.3 collective-permute-done.10
  132.0 8.7 %collective-permute-done.12 = bf16[192,768]{1,0:T(8,128)(2,1)S(1)} collective-permute-done((bf16[192,768]{1,0:T(8,128)(2,1)S(1)}, bf16[192,768]{1,0:T(8,128)(2,1)S(1)}, u32[]{:S(2)}, u32[]{:S(2)}) %collective-permute-start.12) | collective-permute-done | bytes 294944 | tf_op jit(solution)/shard_map/ppermute | solution.py:21
  141.6 13.3 %collective-permute-start.43 = (bf16[192,1152]{1,0:T(8,128)(2,1)S(1)}, bf16[192,1152]{1,0:T(8,128)(2,1)S(1)}, u32[]{:S(2)}, u32[]{:S(2)}) collective-permute-start(bf16[192,1152]{1,0:T(8,128)(2,1)S(1)} %bitcast.323), channel_id=1, source_target_pairs={{0,16},{8,24},{16,0},{24,8},{1,17},{9,25},{17,1},{25,9},{2,18},{10... | collective-permute-start | bytes 1327112 | tf_op jit(solution)/shard_map/ppermute | solution.py:21
  155.0 12.5 %collective-permute-done.37 = bf16[192,1152]{1,0:T(8,128)(2,1)S(1)} collective-permute-done((bf16[192,1152]{1,0:T(8,128)(2,1)S(1)}, bf16[192,1152]{1,0:T(8,128)(2,1)S(1)}, u32[]{:S(2)}, u32[]{:S(2)}) %collective-permute-start.37) | collective-permute-done | bytes 442400 | tf_op jit(solution)/shard_map/ppermute | solution.py:21
  169.4 6.6 %collective-permute-done.42 = bf16[192,1152]{1,0:T(8,128)(2,1)S(1)} collective-permute-done((bf16[192,1152]{1,0:T(8,128)(2,1)S(1)}, bf16[192,1152]{1,0:T(8,128)(2,1)S(1)}, u32[]{:S(2)}, u32[]{:S(2)}) %collective-permute-start.42) | collective-permute-done | bytes 442400 | tf_op jit(solution)/shard_map/ppermute | solution.py:21
  180.8 7.4 %collective-permute-start.29 = (bf16[192,1152]{1,0:T(8,128)(2,1)S(1)}, bf16[192,1152]{1,0:T(8,128)(2,1)S(1)}, u32[]{:S(2)}, u32[]{:S(2)}) collective-permute-start(bf16[192,1152]{1,0:T(8,128)(2,1)S(1)} %copy-done.18), channel_id=1, source_target_pairs={{0,16},{8,24},{16,0},{24,8},{1,17},{9,25},{17,1},{25,9},{2,18},{10... | collective-permute-start | bytes 1327112 | tf_op jit(solution)/shard_map/ppermute | solution.py:21
  190.7 5.6 fusion.2
  206.3 7.5 %collective-permute-done.13.prev_ref = bf16[1024,256]{1,0:T(8,128)(2,1)S(1)} collective-permute-done((bf16[1024,256]{1,0:T(8,128)(2,1)S(1)}, bf16[1024,256]{1,0:T(8,128)(2,1)S(1)}, u32[]{:S(2)}, u32[]{:S(2)}) %collective-permute-start.13) | collective-permute-done | bytes 524320 | tf_op jit(solution)/shard_map/ppermute | solution.py:27
  216.6 9.6 %attend_forward.1 = (bf16[1024,384]{1,0:T(8,128)(2,1)S(1)}, f32[3,1024]{1,0:T(4,128)S(1)}) custom-call(s32[4]{0:T(128)S(1)} %broadcast_xor_fusion.blocks_ref, bf16[1024,384]{1,0:T(8,128)(2,1)S(1)} %convolution_convert_fusion.9.q_ref, bf16[1024,256]{1,0:T(8,128)(2,1)S(1)} %collective-permute-done.13.prev_ref, ...), custom_call_target="tpu_custom_call" | custom-call | flops 1610612736 | bytes 6291456 | tf_op jit(solution)/shard_map/attend_forward/pallas_call | solution.py:209
  232.0 12.2 %collective-permute-done.30 = bf16[192,1152]{1,0:T(8,128)(2,1)S(1)} collective-permute-done((bf16[192,1152]{1,0:T(8,128)(2,1)S(1)}, bf16[192,1152]{1,0:T(8,128)(2,1)S(1)}, u32[]{:S(2)}, u32[]{:S(2)}) %collective-permute-start.30) | collective-permute-done | bytes 442400 | tf_op jit(solution)/shard_map/ppermute | solution.py:21
  250.8 6.5 %collective-permute-done.39 = bf16[192,1152]{1,0:T(8,128)(2,1)S(1)} collective-permute-done((bf16[192,1152]{1,0:T(8,128)(2,1)S(1)}, bf16[192,1152]{1,0:T(8,128)(2,1)S(1)}, u32[]{:S(2)}, u32[]{:S(2)}) %collective-permute-start.39) | collective-permute-done | bytes 442400 | tf_op jit(solution)/shard_map/ppermute | solution.py:21
  257.3 9.2 %collective-permute-done.22 = bf16[256,1536]{1,0:T(8,128)(2,1)S(1)} collective-permute-done((bf16[256,1536]{1,0:T(8,128)(2,1)S(1)}, bf16[256,1536]{1,0:T(8,128)(2,1)S(1)}, u32[]{:S(2)}, u32[]{:S(2)}) %collective-permute-start.22) | collective-permute-done | bytes 786464 | tf_op jit(solution)/shard_map/ppermute | solution.py:21
  268.8 5.8 collective-permute-done.32
  275.4 9.2 %collective-permute-done.23 = bf16[256,1536]{1,0:T(8,128)(2,1)S(1)} collective-permute-done((bf16[256,1536]{1,0:T(8,128)(2,1)S(1)}, bf16[256,1536]{1,0:T(8,128)(2,1)S(1)}, u32[]{:S(2)}, u32[]{:S(2)}) %collective-permute-start.23) | collective-permute-done | bytes 786464 | tf_op jit(solution)/shard_map/ppermute | solution.py:21
  284.6 7.7 %fusion.52 = f32[1024,1152]{1,0:T(8,128)} fusion(bf16[1536,1152]{1,0:T(8,128)(2,1)S(1)} %bitcast.302, bf16[256,1536]{1,0:T(8,128)(2,1)S(1)} %collective-permute-done.51, bf16[256,1536]{1,0:T(8,128)(2,1)} %collective-permute-done.50, bf16[256,1536]{1,0:T(8,128)(2,1)} %collective-permute-done.49, bf16[256,1536]{1,0:T(8,128)(2,1)S(1)} %bitcast.319), kind=kOutput, calls=%fused_computation.129 | convolution fusion | flops 3636461568 | bytes 11403264 | tf_op jit(solution)/shard_map/dot_general | solution.py:92
  292.4 8.0 %fusion.89 = f32[1024,1152]{1,0:T(8,128)} fusion(bf16[1536,1152]{1,0:T(8,128)(2,1)S(1)} %bitcast.299, bf16[256,1536]{1,0:T(8,128)(2,1)S(1)} %collective-permute-done.25, bf16[256,1536]{1,0:T(8,128)(2,1)S(1)} %collective-permute-done.24, bf16[256,1536]{1,0:T(8,128)(2,1)S(1)} %collective-permute-done.23, bf16[256,1536]{1,0:T(8,128)(2,1)S(1)} %multiply_convert_fusion.2), kind=kOutput, calls=%fused_computation.246 | convolution fusion | flops 3636461568 | bytes 11403264 | tf_op jit(solution)/shard_map/dot_general | solution.py:92
  300.4 15.2 %fusion.9 = (bf16[1024,1152]{1,0:T(8,128)(2,1)}, bf16[1024,1152]{1,0:T(8,128)(2,1)}, bf16[1024,1152]{1,0:T(8,128)(2,1)}) fusion(f32[1024,1152]{1,0:T(8,128)} %fusion.52, f32[1024,1152]{1,0:T(8,128)} %fusion.89, bf16[1536,1152]{1,0:T(8,128)(2,1)} %bitcast.38, bf16[256,1536]{1,0:T(8,128)(2,1)S(1)} %collective-permute-done.25, ...), kind=kOutput, calls=%fused_computation.16 | convolution fusion | flops 3667132416 | bytes 23199744 | tf_op jit(solution)/shard_map/dot_general | solution.py:92
  319.3 5.7 convolution_convert_fusion
  329.5 6.2 %convolution_convert_fusion.1 = bf16[1536,1152]{1,0:T(8,128)(2,1)S(1)} fusion(bf16[1024,1152]{1,0:T(8,128)(2,1)} %get-tuple-element.59, bf16[256,1536]{1,0:T(8,128)(2,1)S(1)} %collective-permute-done.25, bf16[256,1536]{1,0:T(8,128)(2,1)S(1)} %collective-permute-done.24, bf16[256,1536]{1,0:T(8,128)(2,1)S(1)} %collective-permute-done.23, ...), kind=kOutput, calls=%fused_computation.3 | convolution fusion | flops 3638231040 | bytes 9043968 | tf_op jit(solution)/shard_map/dot_general | solution.py:294
  338.3 5.5 fusion.12
  344.3 6.4 %convolution_convert_fusion.2 = bf16[1536,1152]{1,0:T(8,128)(2,1)S(1)} fusion(bf16[1024,1152]{1,0:T(8,128)(2,1)} %get-tuple-element.58, bf16[256,1536]{1,0:T(8,128)(2,1)S(1)} %copy-done.33, bf16[256,1536]{1,0:T(8,128)(2,1)S(1)} %copy-done.31, bf16[256,1536]{1,0:T(8,128)(2,1)S(1)} %collective-permute-done.23, bf16[256,1536]{1,0:T(8,128)(2,1)S(1)} %multiply_convert_fusion.2), kind=kOutput, calls=%fused_computation.4 | convolution fusion | flops 3638231040 | bytes 9043968 | tf_op jit(solution)/shard_map/dot_general | solution.py:294
  353.0 3.9 fusion.27
  357.0 4.0 convolution_add_fusion.5
  362.6 6.0 fusion.11
  372.6 5.4 collective-permute-start.83
  378.0 27.9 %collective-permute-done.78 = bf16[4,192,1152]{2,1,0:T(8,128)(2,1)S(1)} collective-permute-done((bf16[4,192,1152]{2,1,0:T(8,128)(2,1)}, bf16[4,192,1152]{2,1,0:T(8,128)(2,1)S(1)}, u32[]{:S(2)}, u32[]{:S(2)}) %collective-permute-start.78) | collective-permute-done | bytes 1769504 | tf_op jit(solution)/shard_map/ppermute | solution.py:21
  405.9 5.5 collective-permute-start.84
  418.2 25.2 %collective-permute-done.74 = bf16[4,192,1152]{2,1,0:T(8,128)(2,1)S(1)} collective-permute-done((bf16[4,192,1152]{2,1,0:T(8,128)(2,1)}, bf16[4,192,1152]{2,1,0:T(8,128)(2,1)S(1)}, u32[]{:S(2)}, u32[]{:S(2)}) %collective-permute-start.74) | collective-permute-done | bytes 1769504 | tf_op jit(solution)/shard_map/ppermute | solution.py:21
  445.4 5.6 collective-permute-start.80
  453.2 9.3 %collective-permute-done.54 = bf16[256,1536]{1,0:T(8,128)(2,1)S(1)} collective-permute-done((bf16[256,1536]{1,0:T(8,128)(2,1)S(1)}, bf16[256,1536]{1,0:T(8,128)(2,1)S(1)}, u32[]{:S(2)}, u32[]{:S(2)}) %collective-permute-start.54) | collective-permute-done | bytes 786464 | tf_op jit(solution)/shard_map/ppermute | solution.py:21
  463.7 5.4 collective-permute-start.75
  469.2 11.9 %collective-permute-done.80 = bf16[192,1152]{1,0:T(8,128)(2,1)S(1)} collective-permute-done((bf16[192,1152]{1,0:T(8,128)(2,1)S(1)}, bf16[192,1152]{1,0:T(8,128)(2,1)S(1)}, u32[]{:S(2)}, u32[]{:S(2)}) %collective-permute-start.80) | collective-permute-done | bytes 442400 | tf_op jit(solution)/shard_map/ppermute | solution.py:21
  484.4 3.9 convolution_convert_fusion.8.dout_ref
  488.3 15.7 %attend_backward.1 = (bf16[1024,384]{1,0:T(8,128)(2,1)S(1)}, bf16[1024,256]{1,0:T(8,128)(2,1)S(1)}, f32[1024,256]{1,0:T(8,128)S(1)}) custom-call(s32[4]{0:T(128)S(1)} %broadcast_xor_fusion.blocks_ref, bf16[1024,384]{1,0:T(8,128)(2,1)S(1)} %convolution_convert_fusion.9.q_ref, bf16[1024,256]{1,0:T(8,128)(2,1)S(1)} %collective-permute-done.13.prev_ref, ...), custom_call_target="tpu_custom_call" | custom-call | flops 4026531840 | bytes 10485760 | tf_op jit(solution)/shard_map/attend_backward/pallas_call | solution.py:242
  505.3 13.6 %collective-permute-done.76 = bf16[192,1152]{1,0:T(8,128)(2,1)S(1)} collective-permute-done((bf16[192,1152]{1,0:T(8,128)(2,1)S(1)}, bf16[192,1152]{1,0:T(8,128)(2,1)S(1)}, u32[]{:S(2)}, u32[]{:S(2)}) %collective-permute-start.76) | collective-permute-done | bytes 442400 | tf_op jit(solution)/shard_map/ppermute | solution.py:21
  532.9 8.8 %collective-permute-done.70 = bf16[4,192,384]{2,1,0:T(8,128)(2,1)S(1)} collective-permute-done((bf16[4,192,384]{2,1,0:T(8,128)(2,1)S(1)}, bf16[4,192,384]{2,1,0:T(8,128)(2,1)S(1)}, u32[]{:S(2)}, u32[]{:S(2)}) %collective-permute-start.70) | collective-permute-done | bytes 589856 | tf_op jit(solution)/shard_map/ppermute | solution.py:21
  541.9 23.8 %collective-permute-start.71 = (bf16[192,384]{1,0:T(8,128)(2,1)S(1)}, bf16[192,384]{1,0:T(8,128)(2,1)S(1)}, u32[]{:S(2)}, u32[]{:S(2)}) collective-permute-start(bf16[192,384]{1,0:T(8,128)(2,1)S(1)} %get-tuple-element.71), channel_id=1, source_target_pairs={{0,8},{8,0},{16,24},{24,16},{1,9},{9,1},{17,25},{25,17},{2,10},{10... | collective-permute-start | bytes 442376 | tf_op jit(solution)/shard_map/ppermute | solution.py:21
  569.6 8.9 %collective-permute-start.61 = (bf16[192,384]{1,0:T(8,128)(2,1)S(1)}, bf16[192,384]{1,0:T(8,128)(2,1)S(1)}, u32[]{:S(2)}, u32[]{:S(2)}) collective-permute-start(bf16[192,384]{1,0:T(8,128)(2,1)S(1)} %get-tuple-element.77), channel_id=1, source_target_pairs={{0,8},{8,0},{16,24},{24,16},{1,9},{9,1},{17,25},{25,17},{2,10},{10... | collective-permute-start | bytes 442376 | tf_op jit(solution)/shard_map/ppermute | solution.py:21
  582.8 8.4 %collective-permute-done.62 = bf16[192,384]{1,0:T(8,128)(2,1)S(1)} collective-permute-done((bf16[192,384]{1,0:T(8,128)(2,1)S(1)}, bf16[192,384]{1,0:T(8,128)(2,1)S(1)}, u32[]{:S(2)}, u32[]{:S(2)}) %collective-permute-start.62) | collective-permute-done | bytes 147488 | tf_op jit(solution)/shard_map/ppermute | solution.py:21
  599.1 8.3 %collective-permute-done.66 = bf16[192,384]{1,0:T(8,128)(2,1)S(1)} collective-permute-done((bf16[192,384]{1,0:T(8,128)(2,1)S(1)}, bf16[192,384]{1,0:T(8,128)(2,1)S(1)}, u32[]{:S(2)}, u32[]{:S(2)}) %collective-permute-start.66) | collective-permute-done | bytes 147488 | tf_op jit(solution)/shard_map/ppermute | solution.py:21
  (342 shorter events, 155.4 us)
Async XLA Ops:
  5.5 17.6 %collective-permute-start.3 = (bf16[1,48,384]{2,1,0:T(8,128)(2,1)S(1)}, bf16[1,48,384]{2,1,0:T(8,128)(2,1)}, u32[]{:S(2)}, u32[]{:S(2)}) collective-permute-start(bf16[1,48,384]{2,1,0:T(8,128)(2,1)S(1)} %get-tuple-element.57), channel_id=1, source_target_pairs={{0,2},{1,3},{2,0},{3,1},{4,6},{5,7},{6,4},{7,5},{8,10},{9,11},{10,... | collective-permute-start | bytes 110600 | tf_op jit(solution)/shard_map/ppermute | solution.py:21
  8.6 17.0 %collective-permute-start.4 = (bf16[1,48,384]{2,1,0:T(8,128)(2,1)S(1)}, bf16[1,48,384]{2,1,0:T(8,128)(2,1)}, u32[]{:S(2)}, u32[]{:S(2)}) collective-permute-start(bf16[1,48,384]{2,1,0:T(8,128)(2,1)S(1)} %get-tuple-element.57), channel_id=1, source_target_pairs={{0,1},{1,0},{2,3},{3,2},{4,5},{5,4},{6,7},{7,6},{8,9},{9,8},{10,11... | collective-permute-start | bytes 110600 | tf_op jit(solution)/shard_map/ppermute | solution.py:21
  8.6 159.5 %collective-permute-start = (bf16[256,1536]{1,0:T(8,128)(2,1)}, bf16[256,1536]{1,0:T(8,128)(2,1)S(1)}, u32[]{:S(2)}, u32[]{:S(2)}) collective-permute-start(bf16[256,1536]{1,0:T(8,128)(2,1)} %bitcast.279), channel_id=1, source_target_pairs={{0,2},{1,3},{2,0},{3,1},{4,6},{5,7},{6,4},{7,5},{8,10},{9,11},{10,... | collective-permute-start | bytes 2359304 | tf_op jit(solution)/shard_map/ppermute | solution.py:21
  8.7 172.0 %collective-permute-start.1 = (bf16[256,1536]{1,0:T(8,128)(2,1)}, bf16[256,1536]{1,0:T(8,128)(2,1)S(1)}, u32[]{:S(2)}, u32[]{:S(2)}) collective-permute-start(bf16[256,1536]{1,0:T(8,128)(2,1)} %bitcast.280), channel_id=1, source_target_pairs={{0,1},{1,0},{2,3},{3,2},{4,5},{5,4},{6,7},{7,6},{8,9},{9,8},{10,11... | collective-permute-start | bytes 2359304 | tf_op jit(solution)/shard_map/ppermute | solution.py:21
  9.1 20.9 %collective-permute-start.14 = (bf16[192,384]{1,0:T(8,128)(2,1)}, bf16[192,384]{1,0:T(8,128)(2,1)}, u32[]{:S(2)}, u32[]{:S(2)}) collective-permute-start(bf16[192,384]{1,0:T(8,128)(2,1)} %bitcast.325), channel_id=1, source_target_pairs={{0,4},{4,0},{1,5},{5,1},{2,6},{6,2},{3,7},{7,3},{8,12},{12,8},{9,1... | collective-permute-start | bytes 442376 | tf_op jit(solution)/shard_map/ppermute | solution.py:21
  40.8 39.0 %collective-permute-start.33 = (bf16[192,1152]{1,0:T(8,128)(2,1)S(1)}, bf16[192,1152]{1,0:T(8,128)(2,1)S(1)}, u32[]{:S(2)}, u32[]{:S(2)}) collective-permute-start(bf16[192,1152]{1,0:T(8,128)(2,1)S(1)} %copy-done.14), channel_id=1, source_target_pairs={{0,4},{4,0},{1,5},{5,1},{2,6},{6,2},{3,7},{7,3},{8,12},{12,8},{9,1... | collective-permute-start | bytes 1327112 | tf_op jit(solution)/shard_map/ppermute | solution.py:21
  42.9 22.0 %collective-permute-start.6 = (bf16[192,768]{1,0:T(8,128)(2,1)S(1)}, bf16[192,768]{1,0:T(8,128)(2,1)S(1)}, u32[]{:S(2)}, u32[]{:S(2)}) collective-permute-start(bf16[192,768]{1,0:T(8,128)(2,1)S(1)} %pad_maximum_fusion.8), channel_id=1, source_target_pairs={{0,4},{4,0},{1,5},{5,1},{2,6},{6,2},{3,7},{7,3},{8,12},{12,8},{9,1... | collective-permute-start | bytes 884744 | tf_op jit(solution)/shard_map/ppermute | solution.py:21
  64.9 21.9 %collective-permute-start.34 = (bf16[192,1152]{1,0:T(8,128)(2,1)S(1)}, bf16[192,1152]{1,0:T(8,128)(2,1)S(1)}, u32[]{:S(2)}, u32[]{:S(2)}) collective-permute-start(bf16[192,1152]{1,0:T(8,128)(2,1)S(1)} %copy-done.14), channel_id=1, source_target_pairs={{0,8},{8,0},{16,24},{24,16},{1,9},{9,1},{17,25},{25,17},{2,10},{10... | collective-permute-start | bytes 1327112 | tf_op jit(solution)/shard_map/ppermute | solution.py:21
  79.5 62.0 %collective-permute-start.36 = (bf16[192,1152]{1,0:T(8,128)(2,1)S(1)}, bf16[192,1152]{1,0:T(8,128)(2,1)S(1)}, u32[]{:S(2)}, u32[]{:S(2)}) collective-permute-start(bf16[192,1152]{1,0:T(8,128)(2,1)S(1)} %copy-done.14), channel_id=1, source_target_pairs={{0,16},{8,24},{16,0},{24,8},{1,17},{9,25},{17,1},{25,9},{2,18},{10... | collective-permute-start | bytes 1327112 | tf_op jit(solution)/shard_map/ppermute | solution.py:21
  126.5 41.1 %collective-permute-start.38 = (bf16[192,1152]{1,0:T(8,128)(2,1)S(1)}, bf16[192,1152]{1,0:T(8,128)(2,1)S(1)}, u32[]{:S(2)}, u32[]{:S(2)}) collective-permute-start(bf16[192,1152]{1,0:T(8,128)(2,1)S(1)} %copy-done.14), channel_id=1, source_target_pairs={{0,24},{8,16},{16,8},{24,0},{1,25},{9,17},{17,9},{25,1},{2,26},{10... | collective-permute-start | bytes 1327112 | tf_op jit(solution)/shard_map/ppermute | solution.py:21
  141.6 38.3 %collective-permute-start.43 = (bf16[192,1152]{1,0:T(8,128)(2,1)S(1)}, bf16[192,1152]{1,0:T(8,128)(2,1)S(1)}, u32[]{:S(2)}, u32[]{:S(2)}) collective-permute-start(bf16[192,1152]{1,0:T(8,128)(2,1)S(1)} %bitcast.323), channel_id=1, source_target_pairs={{0,16},{8,24},{16,0},{24,8},{1,17},{9,25},{17,1},{25,9},{2,18},{10... | collective-permute-start | bytes 1327112 | tf_op jit(solution)/shard_map/ppermute | solution.py:21
  167.6 64.3 %collective-permute-start.45 = (bf16[192,1152]{1,0:T(8,128)(2,1)S(1)}, bf16[192,1152]{1,0:T(8,128)(2,1)S(1)}, u32[]{:S(2)}, u32[]{:S(2)}) collective-permute-start(bf16[192,1152]{1,0:T(8,128)(2,1)S(1)} %bitcast.324), channel_id=1, source_target_pairs={{0,24},{8,16},{16,8},{24,0},{1,25},{9,17},{17,9},{25,1},{2,26},{10... | collective-permute-start | bytes 1327112 | tf_op jit(solution)/shard_map/ppermute | solution.py:21
  168.0 82.5 %collective-permute-start.49 = (bf16[256,1536]{1,0:T(8,128)(2,1)S(1)}, bf16[256,1536]{1,0:T(8,128)(2,1)}, u32[]{:S(2)}, u32[]{:S(2)}) collective-permute-start(bf16[256,1536]{1,0:T(8,128)(2,1)S(1)} %bitcast.317), channel_id=1, source_target_pairs={{0,2},{1,3},{2,0},{3,1},{4,6},{5,7},{6,4},{7,5},{8,10},{9,11},{10,... | collective-permute-start | bytes 2359304 | tf_op jit(solution)/shard_map/ppermute | solution.py:21
  179.9 104.7 %collective-permute-start.50 = (bf16[256,1536]{1,0:T(8,128)(2,1)S(1)}, bf16[256,1536]{1,0:T(8,128)(2,1)}, u32[]{:S(2)}, u32[]{:S(2)}) collective-permute-start(bf16[256,1536]{1,0:T(8,128)(2,1)S(1)} %bitcast.318), channel_id=1, source_target_pairs={{0,1},{1,0},{2,3},{3,2},{4,5},{5,4},{6,7},{7,6},{8,9},{9,8},{10,11... | collective-permute-start | bytes 2359304 | tf_op jit(solution)/shard_map/ppermute | solution.py:21
  180.8 47.4 %collective-permute-start.29 = (bf16[192,1152]{1,0:T(8,128)(2,1)S(1)}, bf16[192,1152]{1,0:T(8,128)(2,1)S(1)}, u32[]{:S(2)}, u32[]{:S(2)}) collective-permute-start(bf16[192,1152]{1,0:T(8,128)(2,1)S(1)} %copy-done.18), channel_id=1, source_target_pairs={{0,16},{8,24},{16,0},{24,8},{1,17},{9,25},{17,1},{25,9},{2,18},{10... | collective-permute-start | bytes 1327112 | tf_op jit(solution)/shard_map/ppermute | solution.py:21
  227.3 18.0 %collective-permute-start.21 = (bf16[512,1536]{1,0:T(8,128)(2,1)S(1)}, bf16[512,1536]{1,0:T(8,128)(2,1)S(1)}, u32[]{:S(2)}, u32[]{:S(2)}) collective-permute-start(bf16[512,1536]{1,0:T(8,128)(2,1)S(1)} %convolution_convert_fusion.4), channel_id=1, source_target_pairs={{0,1},{1,0},{2,3},{3,2},{4,5},{5,4},{6,7},{7,6},{8,9},{9,8},{10,11... | collective-permute-start | bytes 4718600 | tf_op jit(solution)/shard_map/ppermute | solution.py:21
  228.2 20.0 %collective-permute-start.31 = (bf16[192,1152]{1,0:T(8,128)(2,1)S(1)}, bf16[192,1152]{1,0:T(8,128)(2,1)S(1)}, u32[]{:S(2)}, u32[]{:S(2)}) collective-permute-start(bf16[192,1152]{1,0:T(8,128)(2,1)S(1)} %copy-done.18), channel_id=1, source_target_pairs={{0,24},{8,16},{16,8},{24,0},{1,25},{9,17},{17,9},{25,1},{2,26},{10... | collective-permute-start | bytes 1327112 | tf_op jit(solution)/shard_map/ppermute | solution.py:21
  245.3 23.5 %collective-permute-start.46 = (bf16[192,1152]{1,0:T(8,128)(2,1)S(1)}, bf16[192,1152]{1,0:T(8,128)(2,1)S(1)}, u32[]{:S(2)}, u32[]{:S(2)}) collective-permute-start(bf16[192,1152]{1,0:T(8,128)(2,1)S(1)} %collective-permute-done.45), channel_id=1, source_target_pairs={{0,4},{4,0},{1,5},{5,1},{2,6},{6,2},{3,7},{7,3},{8,12},{12,8},{9,1... | collective-permute-start | bytes 1327112 | tf_op jit(solution)/shard_map/ppermute | solution.py:21
  248.1 18.3 %collective-permute-start.22 = (bf16[256,1536]{1,0:T(8,128)(2,1)S(1)}, bf16[256,1536]{1,0:T(8,128)(2,1)S(1)}, u32[]{:S(2)}, u32[]{:S(2)}) collective-permute-start(bf16[256,1536]{1,0:T(8,128)(2,1)S(1)} %slice.245), channel_id=1, source_target_pairs={{0,2},{1,3},{2,0},{3,1},{4,6},{5,7},{6,4},{7,5},{8,10},{9,11},{10,... | collective-permute-start | bytes 2359304 | tf_op jit(solution)/shard_map/ppermute | solution.py:21
  250.5 24.1 %collective-permute-start.32 = (bf16[192,1152]{1,0:T(8,128)(2,1)S(1)}, bf16[192,1152]{1,0:T(8,128)(2,1)S(1)}, u32[]{:S(2)}, u32[]{:S(2)}) collective-permute-start(bf16[192,1152]{1,0:T(8,128)(2,1)S(1)} %collective-permute-done.31), channel_id=1, source_target_pairs={{0,4},{4,0},{1,5},{5,1},{2,6},{6,2},{3,7},{7,3},{8,12},{12,8},{9,1... | collective-permute-start | bytes 1327112 | tf_op jit(solution)/shard_map/ppermute | solution.py:21
  257.3 27.3 %collective-permute-start.51 = (bf16[256,1536]{1,0:T(8,128)(2,1)}, bf16[256,1536]{1,0:T(8,128)(2,1)S(1)}, u32[]{:S(2)}, u32[]{:S(2)}) collective-permute-start(bf16[256,1536]{1,0:T(8,128)(2,1)} %collective-permute-done.49), channel_id=1, source_target_pairs={{0,1},{1,0},{2,3},{3,2},{4,5},{5,4},{6,7},{7,6},{8,9},{9,8},{10,11... | collective-permute-start | bytes 2359304 | tf_op jit(solution)/shard_map/ppermute | solution.py:21
  267.2 17.4 %collective-permute-start.23 = (bf16[256,1536]{1,0:T(8,128)(2,1)S(1)}, bf16[256,1536]{1,0:T(8,128)(2,1)S(1)}, u32[]{:S(2)}, u32[]{:S(2)}) collective-permute-start(bf16[256,1536]{1,0:T(8,128)(2,1)S(1)} %multiply_convert_fusion.2), channel_id=1, source_target_pairs={{0,2},{1,3},{2,0},{3,1},{4,6},{5,7},{6,4},{7,5},{8,10},{9,11},{10,... | collective-permute-start | bytes 2359304 | tf_op jit(solution)/shard_map/ppermute | solution.py:21
  275.4 17.0 %collective-permute-start.24 = (bf16[256,1536]{1,0:T(8,128)(2,1)S(1)}, bf16[256,1536]{1,0:T(8,128)(2,1)S(1)}, u32[]{:S(2)}, u32[]{:S(2)}) collective-permute-start(bf16[256,1536]{1,0:T(8,128)(2,1)S(1)} %multiply_convert_fusion.2), channel_id=1, source_target_pairs={{0,1},{1,0},{2,3},{3,2},{4,5},{5,4},{6,7},{7,6},{8,9},{9,8},{10,11... | collective-permute-start | bytes 2359304 | tf_op jit(solution)/shard_map/ppermute | solution.py:21
  326.3 43.3 %collective-permute-start.82 = (bf16[4,192,1152]{2,1,0:T(8,128)(2,1)}, bf16[4,192,1152]{2,1,0:T(8,128)(2,1)}, u32[]{:S(2)}, u32[]{:S(2)}) collective-permute-start(bf16[4,192,1152]{2,1,0:T(8,128)(2,1)} %dynamic-slice_bitcast_fusion), channel_id=1, source_target_pairs={{0,4},{4,0},{1,5},{5,1},{2,6},{6,2},{3,7},{7,3},{8,12},{12,8},{9,1... | collective-permute-start | bytes 5308424 | tf_op jit(solution)/shard_map/ppermute | solution.py:21
  337.1 68.7 %collective-permute-start.78 = (bf16[4,192,1152]{2,1,0:T(8,128)(2,1)}, bf16[4,192,1152]{2,1,0:T(8,128)(2,1)S(1)}, u32[]{:S(2)}, u32[]{:S(2)}) collective-permute-start(bf16[4,192,1152]{2,1,0:T(8,128)(2,1)} %dynamic-slice_bitcast_fusion.1), channel_id=1, source_target_pairs={{0,4},{4,0},{1,5},{5,1},{2,6},{6,2},{3,7},{7,3},{8,12},{12,8},{9,1... | collective-permute-start | bytes 5308424 | tf_op jit(solution)/shard_map/ppermute | solution.py:21
  338.2 18.7 %collective-permute-start.47 = (bf16[512,1536]{1,0:T(8,128)(2,1)S(1)}, bf16[512,1536]{1,0:T(8,128)(2,1)}, u32[]{:S(2)}, u32[]{:S(2)}) collective-permute-start(bf16[512,1536]{1,0:T(8,128)(2,1)S(1)} %convolution_convert_fusion.3), channel_id=1, source_target_pairs={{0,1},{1,0},{2,3},{3,2},{4,5},{5,4},{6,7},{7,6},{8,9},{9,8},{10,11... | collective-permute-start | bytes 4718600 | tf_op jit(solution)/shard_map/ppermute | solution.py:21
  343.8 18.8 %collective-permute-start.52 = (bf16[512,1536]{1,0:T(8,128)(2,1)}, bf16[512,1536]{1,0:T(8,128)(2,1)}, u32[]{:S(2)}, u32[]{:S(2)}) collective-permute-start(bf16[512,1536]{1,0:T(8,128)(2,1)} %fusion.12), channel_id=1, source_target_pairs={{0,1},{1,0},{2,3},{3,2},{4,5},{5,4},{6,7},{7,6},{8,9},{9,8},{10,11... | collective-permute-start | bytes 4718600 | tf_op jit(solution)/shard_map/ppermute | solution.py:21
  352.1 91.3 %collective-permute-start.74 = (bf16[4,192,1152]{2,1,0:T(8,128)(2,1)}, bf16[4,192,1152]{2,1,0:T(8,128)(2,1)S(1)}, u32[]{:S(2)}, u32[]{:S(2)}) collective-permute-start(bf16[4,192,1152]{2,1,0:T(8,128)(2,1)} %dynamic-slice_bitcast_fusion.2), channel_id=1, source_target_pairs={{0,4},{4,0},{1,5},{5,1},{2,6},{6,2},{3,7},{7,3},{8,12},{12,8},{9,1... | collective-permute-start | bytes 5308424 | tf_op jit(solution)/shard_map/ppermute | solution.py:21
  361.1 53.7 %collective-permute-start.48 = (bf16[256,1536]{1,0:T(8,128)(2,1)S(1)}, bf16[256,1536]{1,0:T(8,128)(2,1)}, u32[]{:S(2)}, u32[]{:S(2)}) collective-permute-start(bf16[256,1536]{1,0:T(8,128)(2,1)S(1)} %slice.244), channel_id=1, source_target_pairs={{0,2},{1,3},{2,0},{3,1},{4,6},{5,7},{6,4},{7,5},{8,10},{9,11},{10,... | collective-permute-start | bytes 2359304 | tf_op jit(solution)/shard_map/ppermute | solution.py:21
  368.7 43.3 %collective-permute-start.53 = (bf16[256,1536]{1,0:T(8,128)(2,1)S(1)}, bf16[256,1536]{1,0:T(8,128)(2,1)S(1)}, u32[]{:S(2)}, u32[]{:S(2)}) collective-permute-start(bf16[256,1536]{1,0:T(8,128)(2,1)S(1)} %slice.243), channel_id=1, source_target_pairs={{0,2},{1,3},{2,0},{3,1},{4,6},{5,7},{6,4},{7,5},{8,10},{9,11},{10,... | collective-permute-start | bytes 2359304 | tf_op jit(solution)/shard_map/ppermute | solution.py:21
  372.6 72.8 %collective-permute-start.83 = (bf16[192,1152]{1,0:T(8,128)(2,1)}, bf16[192,1152]{1,0:T(8,128)(2,1)S(1)}, u32[]{:S(2)}, u32[]{:S(2)}) collective-permute-start(bf16[192,1152]{1,0:T(8,128)(2,1)} %get-tuple-element.61), channel_id=1, source_target_pairs={{0,8},{8,0},{16,24},{24,16},{1,9},{9,1},{17,25},{25,17},{2,10},{10... | collective-permute-start | bytes 1327112 | tf_op jit(solution)/shard_map/ppermute | solution.py:21
  405.9 45.1 %collective-permute-start.84 = (bf16[192,1152]{1,0:T(8,128)(2,1)}, bf16[192,1152]{1,0:T(8,128)(2,1)S(1)}, u32[]{:S(2)}, u32[]{:S(2)}) collective-permute-start(bf16[192,1152]{1,0:T(8,128)(2,1)} %get-tuple-element.63), channel_id=1, source_target_pairs={{0,16},{8,24},{16,0},{24,8},{1,17},{9,25},{17,1},{25,9},{2,18},{10... | collective-permute-start | bytes 1327112 | tf_op jit(solution)/shard_map/ppermute | solution.py:21
  411.9 41.3 %collective-permute-start.85 = (bf16[192,1152]{1,0:T(8,128)(2,1)}, bf16[192,1152]{1,0:T(8,128)(2,1)S(1)}, u32[]{:S(2)}, u32[]{:S(2)}) collective-permute-start(bf16[192,1152]{1,0:T(8,128)(2,1)} %get-tuple-element.62), channel_id=1, source_target_pairs={{0,24},{8,16},{16,8},{24,0},{1,25},{9,17},{17,9},{25,1},{2,26},{10... | collective-permute-start | bytes 1327112 | tf_op jit(solution)/shard_map/ppermute | solution.py:21
  414.8 49.0 %collective-permute-start.79 = (bf16[192,1152]{1,0:T(8,128)(2,1)S(1)}, bf16[192,1152]{1,0:T(8,128)(2,1)S(1)}, u32[]{:S(2)}, u32[]{:S(2)}) collective-permute-start(bf16[192,1152]{1,0:T(8,128)(2,1)S(1)} %get-tuple-element.64), channel_id=1, source_target_pairs={{0,8},{8,0},{16,24},{24,16},{1,9},{9,1},{17,25},{25,17},{2,10},{10... | collective-permute-start | bytes 1327112 | tf_op jit(solution)/shard_map/ppermute | solution.py:21
  443.4 19.2 %collective-permute-start.54 = (bf16[256,1536]{1,0:T(8,128)(2,1)S(1)}, bf16[256,1536]{1,0:T(8,128)(2,1)S(1)}, u32[]{:S(2)}, u32[]{:S(2)}) collective-permute-start(bf16[256,1536]{1,0:T(8,128)(2,1)S(1)} %get-tuple-element.52), channel_id=1, source_target_pairs={{0,2},{1,3},{2,0},{3,1},{4,6},{5,7},{6,4},{7,5},{8,10},{9,11},{10,... | collective-permute-start | bytes 2359304 | tf_op jit(solution)/shard_map/ppermute | solution.py:21
  445.4 35.7 %collective-permute-start.80 = (bf16[192,1152]{1,0:T(8,128)(2,1)S(1)}, bf16[192,1152]{1,0:T(8,128)(2,1)S(1)}, u32[]{:S(2)}, u32[]{:S(2)}) collective-permute-start(bf16[192,1152]{1,0:T(8,128)(2,1)S(1)} %get-tuple-element.66), channel_id=1, source_target_pairs={{0,16},{8,24},{16,0},{24,8},{1,17},{9,25},{17,1},{25,9},{2,18},{10... | collective-permute-start | bytes 1327112 | tf_op jit(solution)/shard_map/ppermute | solution.py:21
  451.0 30.1 %collective-permute-start.81 = (bf16[192,1152]{1,0:T(8,128)(2,1)S(1)}, bf16[192,1152]{1,0:T(8,128)(2,1)S(1)}, u32[]{:S(2)}, u32[]{:S(2)}) collective-permute-start(bf16[192,1152]{1,0:T(8,128)(2,1)S(1)} %get-tuple-element.65), channel_id=1, source_target_pairs={{0,24},{8,16},{16,8},{24,0},{1,25},{9,17},{17,9},{25,1},{2,26},{10... | collective-permute-start | bytes 1327112 | tf_op jit(solution)/shard_map/ppermute | solution.py:21
  453.2 31.2 %collective-permute-start.55 = (bf16[256,1536]{1,0:T(8,128)(2,1)S(1)}, bf16[256,1536]{1,0:T(8,128)(2,1)S(1)}, u32[]{:S(2)}, u32[]{:S(2)}) collective-permute-start(bf16[256,1536]{1,0:T(8,128)(2,1)S(1)} %get-tuple-element.52), channel_id=1, source_target_pairs={{0,1},{1,0},{2,3},{3,2},{4,5},{5,4},{6,7},{7,6},{8,9},{9,8},{10,11... | collective-permute-start | bytes 2359304 | tf_op jit(solution)/shard_map/ppermute | solution.py:21
  462.6 21.8 %collective-permute-start.56 = (bf16[256,1536]{1,0:T(8,128)(2,1)S(1)}, bf16[256,1536]{1,0:T(8,128)(2,1)S(1)}, u32[]{:S(2)}, u32[]{:S(2)}) collective-permute-start(bf16[256,1536]{1,0:T(8,128)(2,1)S(1)} %collective-permute-done.54), channel_id=1, source_target_pairs={{0,1},{1,0},{2,3},{3,2},{4,5},{5,4},{6,7},{7,6},{8,9},{9,8},{10,11... | collective-permute-start | bytes 2359304 | tf_op jit(solution)/shard_map/ppermute | solution.py:21
  463.7 41.6 %collective-permute-start.75 = (bf16[192,1152]{1,0:T(8,128)(2,1)S(1)}, bf16[192,1152]{1,0:T(8,128)(2,1)S(1)}, u32[]{:S(2)}, u32[]{:S(2)}) collective-permute-start(bf16[192,1152]{1,0:T(8,128)(2,1)S(1)} %get-tuple-element.67), channel_id=1, source_target_pairs={{0,8},{8,0},{16,24},{24,16},{1,9},{9,1},{17,25},{25,17},{2,10},{10... | collective-permute-start | bytes 1327112 | tf_op jit(solution)/shard_map/ppermute | solution.py:21
  481.1 37.9 %collective-permute-start.76 = (bf16[192,1152]{1,0:T(8,128)(2,1)S(1)}, bf16[192,1152]{1,0:T(8,128)(2,1)S(1)}, u32[]{:S(2)}, u32[]{:S(2)}) collective-permute-start(bf16[192,1152]{1,0:T(8,128)(2,1)S(1)} %get-tuple-element.69), channel_id=1, source_target_pairs={{0,16},{8,24},{16,0},{24,8},{1,17},{9,25},{17,1},{25,9},{2,18},{10... | collective-permute-start | bytes 1327112 | tf_op jit(solution)/shard_map/ppermute | solution.py:21
  481.1 37.9 %collective-permute-start.77 = (bf16[192,1152]{1,0:T(8,128)(2,1)S(1)}, bf16[192,1152]{1,0:T(8,128)(2,1)S(1)}, u32[]{:S(2)}, u32[]{:S(2)}) collective-permute-start(bf16[192,1152]{1,0:T(8,128)(2,1)S(1)} %get-tuple-element.68), channel_id=1, source_target_pairs={{0,24},{8,16},{16,8},{24,0},{1,25},{9,17},{17,9},{25,1},{2,26},{10... | collective-permute-start | bytes 1327112 | tf_op jit(solution)/shard_map/ppermute | solution.py:21
  504.0 17.3 %collective-permute-start.57 = (bf16[1024,256]{1,0:T(8,128)(2,1)S(1)}, bf16[1024,256]{1,0:T(8,128)(2,1)S(1)}, u32[]{:S(2)}, u32[]{:S(2)}) collective-permute-start(bf16[1024,256]{1,0:T(8,128)(2,1)S(1)} %get-tuple-element.18), channel_id=1, source_target_pairs={{4,0},{5,1},{6,2},{7,3},{12,8},{13,9},{14,10},{15,11},{20,16},{21,... | collective-permute-start | bytes 1572872 | tf_op jit(solution)/shard_map/ppermute | solution.py:27
  525.4 16.3 %collective-permute-start.70 = (bf16[4,192,384]{2,1,0:T(8,128)(2,1)S(1)}, bf16[4,192,384]{2,1,0:T(8,128)(2,1)S(1)}, u32[]{:S(2)}, u32[]{:S(2)}) collective-permute-start(bf16[4,192,384]{2,1,0:T(8,128)(2,1)S(1)} %dynamic-slice_bitcast_fusion.3), channel_id=1, source_target_pairs={{0,4},{4,0},{1,5},{5,1},{2,6},{6,2},{3,7},{7,3},{8,12},{12,8},{9,1... | collective-permute-start | bytes 1769480 | tf_op jit(solution)/shard_map/ppermute | solution.py:21
  527.7 40.5 %collective-permute-start.60 = (bf16[4,192,384]{2,1,0:T(8,128)(2,1)S(1)}, bf16[4,192,384]{2,1,0:T(8,128)(2,1)S(1)}, u32[]{:S(2)}, u32[]{:S(2)}) collective-permute-start(bf16[4,192,384]{2,1,0:T(8,128)(2,1)S(1)} %dynamic-slice_bitcast_fusion.4), channel_id=1, source_target_pairs={{0,4},{4,0},{1,5},{5,1},{2,6},{6,2},{3,7},{7,3},{8,12},{12,8},{9,1... | collective-permute-start | bytes 1769480 | tf_op jit(solution)/shard_map/ppermute | solution.py:21
  531.3 37.0 %collective-permute-start.59 = (bf16[256,1536]{1,0:T(8,128)(2,1)S(1)}, bf16[256,1536]{1,0:T(8,128)(2,1)S(1)}, u32[]{:S(2)}, u32[]{:S(2)}) collective-permute-start(bf16[256,1536]{1,0:T(8,128)(2,1)S(1)} %slice.242), channel_id=1, source_target_pairs={{0,2},{1,3},{2,0},{3,1},{4,6},{5,7},{6,4},{7,5},{8,10},{9,11},{10,... | collective-permute-start | bytes 2359304 | tf_op jit(solution)/shard_map/ppermute | solution.py:21
  541.9 36.6 %collective-permute-start.71 = (bf16[192,384]{1,0:T(8,128)(2,1)S(1)}, bf16[192,384]{1,0:T(8,128)(2,1)S(1)}, u32[]{:S(2)}, u32[]{:S(2)}) collective-permute-start(bf16[192,384]{1,0:T(8,128)(2,1)S(1)} %get-tuple-element.71), channel_id=1, source_target_pairs={{0,8},{8,0},{16,24},{24,16},{1,9},{9,1},{17,25},{25,17},{2,10},{10... | collective-permute-start | bytes 442376 | tf_op jit(solution)/shard_map/ppermute | solution.py:21
  569.5 22.5 %collective-permute-start.64 = (bf16[4,192,384]{2,1,0:T(8,128)(2,1)S(1)}, bf16[4,192,384]{2,1,0:T(8,128)(2,1)S(1)}, u32[]{:S(2)}, u32[]{:S(2)}) collective-permute-start(bf16[4,192,384]{2,1,0:T(8,128)(2,1)S(1)} %fusion.49), channel_id=1, source_target_pairs={{0,4},{4,0},{1,5},{5,1},{2,6},{6,2},{3,7},{7,3},{8,12},{12,8},{9,1... | collective-permute-start | bytes 1769480 | tf_op jit(solution)/shard_map/ppermute | solution.py:21
  (76 other events, 1020.8 us)

commit v2 on v1

--- a/solution.py
+++ b/solution.py
@@ -38,8 +38,12 @@
     return order
 
 
-def gather_tensor(value):
-    pieces = [value]
+def after(value, *deps):
+    return lax.optimization_barrier((value,) + deps)[0]
+
+
+def gather_tensor(value, *deps):
+    pieces = [after(value, *deps) if deps else value]
     for bit in reversed(bits_of(lax.axis_size("tensor"))):
         pieces = pieces + [swap(p, "tensor", bit) for p in pieces]
     return jnp.concatenate(pieces, axis=0)
@@ -58,30 +62,73 @@
     return total
 
 
-def gather_weight(shard):
+def gather_fsdp(shard):
+    nf, f = lax.axis_size("fsdp"), lax.axis_index("fsdp")
+    whole = jnp.zeros((nf,) + shard.shape, shard.dtype)
+    whole = lax.dynamic_update_index_in_dim(whole, shard, f, 0)
+    for k in range(1, nf):
+        whole = lax.dynamic_update_index_in_dim(whole, swap(shard, "fsdp", k), f ^ k, 0)
+    return whole
+
+
+def gather_context(part):
+    nc, c = lax.axis_size("context"), lax.axis_index("context")
+    return [part] + [swap(part, "context", k) for k in range(1, nc)]
+
+
+def join_context(parts):
+    nc, c = lax.axis_size("context"), lax.axis_index("context")
+    nf, rows, n = parts[0].shape
+    whole = jnp.zeros((nf, nc, rows, n), parts[0].dtype)
+    for k, part in enumerate(parts):
+        whole = lax.dynamic_update_index_in_dim(whole, part, c ^ k, 1)
+    return whole.reshape(nf * nc * rows, n)
+
+
+def gather_weights(shards):
+    done, along, parts = (), [], []
+    for s in range(len(shards) + 1):
+        new = ()
+        if s < len(shards):
+            shard = after(shards[s], *done) if done else shards[s]
+            along.append(gather_fsdp(shard))
+            new += (along[s],)
+        if s > 0:
+            part = after(along[s - 1], *done)
+            parts.append(gather_context(part))
+            new += tuple(parts[s - 1][1:])
+        done = new
+    return [join_context(p) for p in parts]
+
+
+class Scatter:
+    def __init__(self):
+        self.last_c, self.last_f = (), ()
+
+    def __call__(self, slabs):
+        nf, nc = lax.axis_size("fsdp"), lax.axis_size("context")
+        f, c = lax.axis_index("fsdp"), lax.axis_index("context")
+        total = lax.dynamic_index_in_dim(slabs, c, 1, False).astype(F32)
+        got = []
+        for k in range(1, nc):
+            sent = lax.dynamic_index_in_dim(slabs, c ^ k, 1, False)
+            got.append(swap(after(sent, *self.last_c) if self.last_c else sent, "context", k))
+            total = total + got[-1].astype(F32)
+        self.last_c = tuple(got)
+        own = lax.dynamic_index_in_dim(total, f, 0, False)
+        sent = tuple(lax.dynamic_index_in_dim(total, f ^ k, 0, False).astype(BF) for k in range(1, nf))
+        if self.last_f:
+            sent = lax.optimization_barrier((sent, self.last_f))[0]
+        got = tuple(swap(x, "fsdp", k + 1) for k, x in enumerate(sent))
+        self.last_f = got
+        for x in got:
+            own = own + x.astype(F32)
+        return own
+
+
+def slabs_of(part):
     nf, nc = lax.axis_size("fsdp"), lax.axis_size("context")
-    f, c = lax.axis_index("fsdp"), lax.axis_index("context")
-    along = [shard] + [swap(shard, "fsdp", k) for k in range(1, nf)]
-    whole = jnp.zeros((nf * nc,) + shard.shape, shard.dtype)
-    for kf in range(nf):
-        for kc in range(nc):
-            piece = along[kf] if kc == 0 else swap(along[kf], "context", kc)
-            whole = lax.dynamic_update_index_in_dim(whole, piece, (f ^ kf) * nc + (c ^ kc), 0)
-    return whole.reshape(nf * nc * shard.shape[0], shard.shape[1])
-
-
-def scatter_grad(part):
-    nf, nc = lax.axis_size("fsdp"), lax.axis_size("context")
-    f, c = lax.axis_index("fsdp"), lax.axis_index("context")
-    slabs = part.reshape(nf, nc, part.shape[0] // (nf * nc), part.shape[1])
-    total = lax.dynamic_index_in_dim(slabs, c, 1, False).astype(F32)
-    for k in range(1, nc):
-        total = total + swap(lax.dynamic_index_in_dim(slabs, c ^ k, 1, False), "context", k).astype(F32)
-    own = lax.dynamic_index_in_dim(total, f, 0, False)
-    for k in range(1, nf):
-        sent = lax.dynamic_index_in_dim(total, f ^ k, 0, False).astype(BF)
-        own = own + swap(sent, "fsdp", k).astype(F32)
-    return own
+    return part.reshape(nf, nc, part.shape[0] // (nf * nc), part.shape[1])
 
 
 def dot_nt(a, b):
@@ -305,26 +352,24 @@
     order = tensor_order(nt)
     blocks = jnp.array(order, jnp.int32) ^ t
 
-    token_rows = gather_tensor(tokens)
-    cot_rows = gather_tensor(cotangent)
-
     part = w_keyval.shape[0]
     kv_cols = w_keyval.shape[1]
+    qcols = w_query.shape[1]
     small = jnp.concatenate([w_keyval, norm_gains.T, jnp.zeros((part, 126), BF)], axis=1)
     pieces = gather_tensor(small[None])
     small = jnp.zeros_like(pieces)
     for i in range(nt):
         small = lax.dynamic_update_index_in_dim(small, pieces[i], blocks[i], 0)
     small = small.reshape(nt * part, small.shape[2])
-    first = gather_weight(jnp.concatenate([w_query, small], axis=1))
-    qcols = w_query.shape[1]
+
+    token_rows = gather_tensor(tokens, pieces)
+    cot_rows = gather_tensor(cotangent, token_rows)
+
+    wo_t, first, wg, wu, wd_t = gather_weights([w_out.T, jnp.concatenate([w_query, small], axis=1), w_gate, w_up, w_down.T])
     wq, wkv = first[:, :qcols], first[:, qcols : qcols + kv_cols]
-    gains = first[:, qcols + kv_cols : qcols + kv_cols + 2].T.astype(F32)
+    gain_cols = first[:, qcols + kv_cols : qcols + kv_cols + 2].astype(F32)
+    gains = gain_cols.T
     gain_one, gain_two = gains[0:1], gains[1:2]
-    wo_t = gather_weight(w_out.T)
-    wg = gather_weight(w_gate)
-    wu = gather_weight(w_up)
-    wd_t = gather_weight(w_down.T)
 
     ids = segment_ids[0]
     own_seg = lax.dynamic_slice_in_dim(ids, c * rows, rows, 0)
@@ -347,40 +392,46 @@
     normed_two = (middle * inv_two * gain_two).astype(BF)
     second_rows = gather_tensor(normed_two)
 
+    scatter = Scatter()
     gate_pre = mm(second_rows, wg)
     up_pre = mm(second_rows, wu)
     activated, gelu_back = jax.vjp(lambda g: jax.nn.gelu(g, approximate=True), gate_pre)
     hidden = (activated * up_pre).astype(BF)
-    grad_down = scatter_grad(mm_tn(cot_rows, hidden).astype(BF)).T
+    grad_down = scatter(slabs_of(mm_tn(cot_rows, hidden).astype(BF))).T
     d_hidden = mm(cot_rows, wd_t)
     d_gate = gelu_back(d_hidden * up_pre)[0].astype(BF)
     d_up = (d_hidden * activated).astype(BF)
-    grad_gate = scatter_grad(mm_tn(second_rows, d_gate).astype(BF))
-    grad_up = scatter_grad(mm_tn(second_rows, d_up).astype(BF))
+    grad_gate = scatter(slabs_of(mm_tn(second_rows, d_gate).astype(BF)))
+    grad_up = scatter(slabs_of(mm_tn(second_rows, d_up).astype(BF)))
     d_two = reduce_tensor(lambda i, j: dot_nt(d_gate[i:j], wg) + dot_nt(d_up[i:j], wu), rows)
-    ffn = reduce_tensor(lambda i, j: dot_nt(hidden[i:j], wd_t), rows)
-    output = (middle + ffn).astype(BF)
 
     gain_two_part = jnp.sum(d_two * middle * inv_two, axis=0, keepdims=True)
     d_middle = cotangent.astype(F32) + norm_backward(d_two, middle, inv_two, gain_two)
     back_rows = gather_tensor(d_middle.astype(BF))
-    grad_out = scatter_grad(mm_tn(back_rows, heads_out).astype(BF)).T
+    ffn = reduce_tensor(lambda i, j: dot_nt(after(hidden, back_rows)[i:j], wd_t), rows)
+    output = (middle + ffn).astype(BF)
+    grad_out = scatter(slabs_of(mm_tn(back_rows, heads_out).astype(BF))).T
     d_head = mm(back_rows, wo_t).astype(BF)
     dq, dprev, dkv = attention_backward(blocks, queries, earlier, keyvals, qseg, kseg, d_head, lse, nt)
     dkv = (dkv + shift(dprev, "context", -1).astype(F32)).astype(BF)
-    grad_query = scatter_grad(mm_tn(normed_one, dq).astype(BF))
     d_one = reduce_tensor(lambda i, j: dot_nt(dq[i:j], wq) + dot_nt(dkv[i:j], wkv), rows)
     inv_one = rms_inverse(own_in)
-    gain_one_part = jnp.sum(d_one * own_in * inv_one, axis=0, keepdims=True)
     input_grad = d_middle + norm_backward(d_one, own_in, inv_one, gain_one)
 
-    gains_part = jnp.concatenate([gain_one_part, gain_two_part, jnp.zeros((126, width), F32)], axis=0).T
-    small_part = jnp.concatenate([mm_tn(normed_one, dkv), gains_part], axis=1).astype(BF)
-    mine = scatter_grad(small_part).reshape(nt, part, kv_cols + 128)
-    mine = jnp.stack([lax.dynamic_index_in_dim(mine, blocks[i], 0, False) for i in range(nt)])
-    mine = reduce_tensor(lambda i, j: mine[i:j], nt)[0]
-    grad_keyval = mine[:, :kv_cols]
-    grad_gains = mine[:, kv_cols : kv_cols + 2].T
+    query_part = mm_tn(normed_one, dq)
+    kv_part = mm_tn(normed_one, dkv)
+    gain_one_part = jnp.sum(query_part * wq.astype(F32), axis=1, keepdims=True) + jnp.sum(kv_part * wkv.astype(F32), axis=1, keepdims=True)
+    gain_one_part = gain_one_part / gain_cols[:, 0:1]
+    small_part = jnp.concatenate([kv_part, gain_one_part, gain_two_part.T, jnp.zeros((width, 126), F32)], axis=1)
+    small_part = small_part.reshape(-1, nt, part, kv_cols + 128)
+    small_part = jnp.stack([lax.dynamic_index_in_dim(small_part, blocks[i], 1, False) for i in range(nt)])
+    small_part = reduce_tensor(lambda i, j: small_part[i:j], nt)[0].astype(BF)
+    nf, nc = lax.axis_size("fsdp"), lax.axis_size("context")
+    last = jnp.concatenate([slabs_of(query_part.astype(BF)), small_part.reshape(nf, nc, part, kv_cols + 128)], axis=2)
+    last = scatter(last)
+    grad_query, small_sum = last[: nt * part], last[nt * part :]
+    grad_keyval = small_sum[:, :kv_cols]
+    grad_gains = small_sum[:, kv_cols : kv_cols + 2].T
     return (output[None], input_grad[None], grad_query, grad_keyval, grad_out, grad_gate, grad_up, grad_down, grad_gains)
 
 

time: 623 us -> 517 us (0.83)
  starting transfers between devices: 146 us -> 89.1 us
  waiting for transfers between devices: 287 us -> 250 us
  local copies, waits for them, and re-layouts: 31.3 us -> 23.2 us
    ppermute x84 -> x65, waiting for transfers between devices: 280 us -> 214 us  [swap(): return lax.ppermute(value, axis, [(i, i ^ k) for i in range(count)])]
    ppermute x84 -> x65, starting transfers between devices: 141 us -> 84.3 us  [swap(): return lax.ppermute(value, axis, [(i, i ^ k) for i in range(count)])]
    ppermute x2, waiting for transfers between devices: 7.53 us -> 36.6 us  [shift(): lax.ppermute(value, axis, [(i, i + steps) for i in range(leading, last)])]
    dynamic_update_slice x39 -> x30, local copies, waits for them, and re-layouts: 14.1 us -> 3.73 us  [the longest x10 2.04 us: join_context(): whole = lax.dynamic_update_index_in_dim(whole, part, c ^ k, 1)]
  transfers between devices with their start and end apart: 86 -> 67, of which waited for: 35 -> 31; matrix products, arithmetic and copies ran while one was open for 17% -> 19% of each run, Pallas kernels for 4% -> 5%
where the time goes in v2:
time: 517 us; the launch traced here: 510 us
  waiting for transfers between devices  250 us (48%)
  starting transfers between devices  89.1 us (17%)
  matrix products  86.2 us (17%)
  other arithmetic  25.6 us (5%)
  Pallas kernels  25.1 us (5%)
  local copies, waits for them, and re-layouts  23.2 us (4%)
  between operations  10.4 us (2%)
    ppermute x65, waiting for transfers between devices, swap(): return lax.ppermute(value, axis, [(i, i ^ k) for i in range(count)])  214 us
    ppermute x65, starting transfers between devices, swap(): return lax.ppermute(value, axis, [(i, i ^ k) for i in range(count)])  84.3 us
    ppermute x2, waiting for transfers between devices, shift(): lax.ppermute(value, axis, [(i, i + steps) for i in range(leading, last)])  36.6 us
    dot_general x6, matrix products, dot_nn(): lax.dot_general(a, b, (((1,), (0,)), ((), ())), preferred_element_type=F32)  32.9 us
    dot_general x12, matrix products, dot_nt(): lax.dot_general(a, b, (((1,), (1,)), ((), ())), preferred_element_type=F32)  27.6 us
    dot_general x6, matrix products, mm_tn(): lax.dot_general(a, b, (((0,), (0,)), ((), ())), preferred_element_type=F32)  25.6 us
    pallas_call x1, Pallas kernels, attention_backward(): pl.pallas_call(attend_backward, grid_spec=pltpu.PrefetchScalarGridSpec(nu...  15.6 us
  transfers between devices with their start and end apart: 67, of which 31 were waited for; matrix products, arithmetic and copies ran while one was open for 19% of the time, Pallas kernels for 5%

profile of v2, /device:TPU:0, one launch (start us, length us, event | category | flops | bytes accessed | tf_op | source)
XLA Modules:
  0.0 509.8 jit_solution(10337294371741667095)
XLA Ops:
  5.5 3.0 collective-permute-start.3
  10.1 2.6 collective-permute-start.7
  24.3 3.1 collective-permute-start.9
  30.2 9.1 %collective-permute-done.9 = bf16[192,768]{1,0:T(8,128)(2,1)S(1)} collective-permute-done((bf16[192,768]{1,0:T(8,128)(2,1)S(1)}, bf16[192,768]{1,0:T(8,128)(2,1)S(1)}, u32[]{:S(2)}, u32[]{:S(2)}) %collective-permute-start.9) | collective-permute-done | bytes 294944 | tf_op jit(solution)/shard_map/ppermute | solution.py:21
  40.8 10.0 %collective-permute-done.10 = bf16[192,768]{1,0:T(8,128)(2,1)S(1)} collective-permute-done((bf16[192,768]{1,0:T(8,128)(2,1)S(1)}, bf16[192,768]{1,0:T(8,128)(2,1)S(1)}, u32[]{:S(2)}, u32[]{:S(2)}) %collective-permute-start.10) | collective-permute-done | bytes 294944 | tf_op jit(solution)/shard_map/ppermute | solution.py:21
  53.3 2.7 collective-permute-start.20
  60.6 11.8 %collective-permute-done.20 = bf16[192,1152]{1,0:T(8,128)(2,1)S(1)} collective-permute-done((bf16[192,1152]{1,0:T(8,128)(2,1)S(1)}, bf16[192,1152]{1,0:T(8,128)(2,1)S(1)}, u32[]{:S(2)}, u32[]{:S(2)}) %collective-permute-start.20) | collective-permute-done | bytes 442400 | tf_op jit(solution)/shard_map/ppermute | solution.py:21
  72.5 16.4 %collective-permute-done.21 = bf16[192,1152]{1,0:T(8,128)(2,1)S(1)} collective-permute-done((bf16[192,1152]{1,0:T(8,128)(2,1)S(1)}, bf16[192,1152]{1,0:T(8,128)(2,1)S(1)}, u32[]{:S(2)}, u32[]{:S(2)}) %collective-permute-start.21) | collective-permute-done | bytes 442400 | tf_op jit(solution)/shard_map/ppermute | solution.py:21
  91.2 7.4 %collective-permute-start.24 = (bf16[192,1152]{1,0:T(8,128)(2,1)S(1)}, bf16[192,1152]{1,0:T(8,128)(2,1)S(1)}, u32[]{:S(2)}, u32[]{:S(2)}) collective-permute-start(bf16[192,1152]{1,0:T(8,128)(2,1)S(1)} %copy-done.29), channel_id=1, source_target_pairs={{0,8},{8,0},{16,24},{24,16},{1,9},{9,1},{17,25},{25,17},{2,10},{10... | collective-permute-start | bytes 1327112 | tf_op jit(solution)/shard_map/ppermute | solution.py:21
  106.9 11.9 %collective-permute-done.24 = bf16[192,1152]{1,0:T(8,128)(2,1)S(1)} collective-permute-done((bf16[192,1152]{1,0:T(8,128)(2,1)S(1)}, bf16[192,1152]{1,0:T(8,128)(2,1)S(1)}, u32[]{:S(2)}, u32[]{:S(2)}) %collective-permute-start.24) | collective-permute-done | bytes 442400 | tf_op jit(solution)/shard_map/ppermute | solution.py:21
  121.5 3.3 collective-permute-start.14
  125.0 7.8 %collective-permute-done.26 = bf16[192,1152]{1,0:T(8,128)(2,1)S(1)} collective-permute-done((bf16[192,1152]{1,0:T(8,128)(2,1)S(1)}, bf16[192,1152]{1,0:T(8,128)(2,1)S(1)}, u32[]{:S(2)}, u32[]{:S(2)}) %collective-permute-start.26) | collective-permute-done | bytes 442400 | tf_op jit(solution)/shard_map/ppermute | solution.py:21
  132.9 17.7 %collective-permute-done.14.prev_ref = bf16[1024,256]{1,0:T(8,128)(2,1)S(1)} collective-permute-done((bf16[1024,256]{1,0:T(8,128)(2,1)S(1)}, bf16[1024,256]{1,0:T(8,128)(2,1)S(1)}, u32[]{:S(2)}, u32[]{:S(2)}) %collective-permute-start.14) | collective-permute-done | bytes 524320 | tf_op jit(solution)/shard_map/ppermute | solution.py:27
  150.9 9.5 %attend_forward.1 = (bf16[1024,384]{1,0:T(8,128)(2,1)S(1)}, f32[3,1024]{1,0:T(4,128)S(1)}) custom-call(s32[4]{0:T(128)S(1)} %broadcast_xor_fusion.blocks_ref, bf16[1024,384]{1,0:T(8,128)(2,1)S(1)} %convolution_convert_fusion.7.q_ref, bf16[1024,256]{1,0:T(8,128)(2,1)S(1)} %collective-permute-done.14.prev_ref, ...), custom_call_target="tpu_custom_call" | custom-call | flops 1610612736 | bytes 6291456 | tf_op jit(solution)/shard_map/attend_forward/pallas_call | solution.py:256
  164.7 2.4 collective-permute-start.33
  167.1 2.5 collective-permute-start.27
  172.8 9.6 %collective-permute-done.31 = bf16[192,1152]{1,0:T(8,128)(2,1)S(1)} collective-permute-done((bf16[192,1152]{1,0:T(8,128)(2,1)S(1)}, bf16[192,1152]{1,0:T(8,128)(2,1)S(1)}, u32[]{:S(2)}, u32[]{:S(2)}) %collective-permute-start.31) | collective-permute-done | bytes 442400 | tf_op jit(solution)/shard_map/ppermute | solution.py:21
  182.5 7.2 %collective-permute-done.16 = bf16[256,1536]{1,0:T(8,128)(2,1)S(1)} collective-permute-done((bf16[256,1536]{1,0:T(8,128)(2,1)S(1)}, bf16[256,1536]{1,0:T(8,128)(2,1)S(1)}, u32[]{:S(2)}, u32[]{:S(2)}) %collective-permute-start.16) | collective-permute-done | bytes 786464 | tf_op jit(solution)/shard_map/ppermute | solution.py:21
  191.2 6.1 %collective-permute-done.32 = bf16[192,1152]{1,0:T(8,128)(2,1)S(1)} collective-permute-done((bf16[192,1152]{1,0:T(8,128)(2,1)S(1)}, bf16[192,1152]{1,0:T(8,128)(2,1)S(1)}, u32[]{:S(2)}, u32[]{:S(2)}) %collective-permute-start.32) | collective-permute-done | bytes 442400 | tf_op jit(solution)/shard_map/ppermute | solution.py:21
  197.5 9.6 %collective-permute-done.27 = bf16[4,192,1152]{2,1,0:T(8,128)(2,1)S(1)} collective-permute-done((bf16[4,192,1152]{2,1,0:T(8,128)(2,1)S(1)}, bf16[4,192,1152]{2,1,0:T(8,128)(2,1)S(1)}, u32[]{:S(2)}, u32[]{:S(2)}) %collective-permute-start.27) | collective-permute-done | bytes 1769504 | tf_op jit(solution)/shard_map/ppermute | solution.py:21
  211.1 7.9 %fusion.88 = f32[1024,1152]{1,0:T(8,128)} fusion(bf16[1536,1152]{1,0:T(8,128)(2,1)S(1)} %bitcast.284, bf16[256,1536]{1,0:T(8,128)(2,1)S(1)} %collective-permute-done.19, bf16[256,1536]{1,0:T(8,128)(2,1)S(1)} %collective-permute-done.18, bf16[256,1536]{1,0:T(8,128)(2,1)S(1)} %collective-permute-done.17, bf16[256,1536]{1,0:T(8,128)(2,1)S(1)} %multiply_convert_fusion.2), kind=kOutput, calls=%fused_computation.228 | convolution fusion | flops 3636461568 | bytes 11403264 | tf_op jit(solution)/shard_map/dot_general | solution.py:139
  219.1 26.6 %collective-permute-done.34 = bf16[4,192,1152]{2,1,0:T(8,128)(2,1)S(1)} collective-permute-done((bf16[4,192,1152]{2,1,0:T(8,128)(2,1)S(1)}, bf16[4,192,1152]{2,1,0:T(8,128)(2,1)S(1)}, u32[]{:S(2)}, u32[]{:S(2)}) %collective-permute-start.34) | collective-permute-done | bytes 1769504 | tf_op jit(solution)/shard_map/ppermute | solution.py:21
  246.1 5.8 %fusion.92 = f32[1024,1152]{1,0:T(8,128)} fusion(bf16[1024,1536]{1,0:T(8,128)(2,1)S(1)} %constant_dynamic-update-slice_fusion.4, bf16[1536,1152]{1,0:T(8,128)(2,1)S(1)} %bitcast.278), kind=kOutput, calls=%fused_computation.232 | convolution fusion | flops 3623878656 | bytes 11403264 | tf_op jit(solution)/shard_map/dot_general | solution.py:139
  251.9 14.5 %fusion.9 = (bf16[1024,1152]{1,0:T(8,128)(2,1)}, bf16[1024,1152]{1,0:T(8,128)(2,1)}, bf16[1024,1152]{1,0:T(8,128)(2,1)}) fusion(f32[1024,1152]{1,0:T(8,128)} %fusion.92, f32[1024,1152]{1,0:T(8,128)} %fusion.88, bf16[1536,1152]{1,0:T(8,128)(2,1)S(1)} %bitcast.281, bf16[256,1536]{1,0:T(8,128)(2,1)S(1)} %copy-done.42, bf16[256,1536]{1,0:T(8,128)(2,1)S(1)} %copy-done.39, ...), kind=kOutput, calls=%fused_computation.16 | convolution fusion | flops 3667132416 | bytes 23199744 | tf_op jit(solution)/shard_map/dot_general | solution.py:139
  266.4 6.2 %convolution_convert_fusion = bf16[1536,1152]{1,0:T(8,128)(2,1)S(1)} fusion(bf16[1024,1536]{1,0:T(8,128)(2,1)S(1)} %copy-done.34, bf16[1024,1152]{1,0:T(8,128)(2,1)} %get-tuple-element.52), kind=kOutput, calls=%fused_computation.2 | convolution fusion | flops 3625648128 | bytes 9043968 | tf_op jit(solution)/shard_map/dot_general | solution.py:341
  278.9 6.2 %convolution_convert_fusion.1 = bf16[1536,1152]{1,0:T(8,128)(2,1)S(1)} fusion(bf16[1024,1152]{1,0:T(8,128)(2,1)} %get-tuple-element.114, bf16[256,1536]{1,0:T(8,128)(2,1)S(1)} %copy-done.43, bf16[256,1536]{1,0:T(8,128)(2,1)S(1)} %copy-done.40, bf16[256,1536]{1,0:T(8,128)(2,1)S(1)} %copy-done.37, bf16[256,1536]{1,0:T(8,128)(2,1)S(1)} %copy-done.26), kind=kOutput, calls=%fused_computation.3 | convolution fusion | flops 3638231040 | bytes 9043968 | tf_op jit(solution)/shard_map/dot_general | solution.py:341
  285.2 6.1 %fusion.26 = f32[512,1536]{1,0:T(8,128)} fusion(bf16[1536,1152]{1,0:T(8,128)(2,1)S(1)} %bitcast.286, bf16[1024,1152]{1,0:T(8,128)(2,1)} %get-tuple-element.115), kind=kOutput, calls=%fused_computation.88 | convolution fusion | flops 1811939328 | bytes 7864320 | tf_op jit(solution)/shard_map/dot_general | solution.py:135
  292.6 6.5 %convolution_convert_fusion.2 = bf16[1536,1152]{1,0:T(8,128)(2,1)S(1)} fusion(bf16[1024,1152]{1,0:T(8,128)(2,1)} %get-tuple-element.115, bf16[256,1536]{1,0:T(8,128)(2,1)S(1)} %copy-done.43, bf16[256,1536]{1,0:T(8,128)(2,1)S(1)} %copy-done.40, bf16[256,1536]{1,0:T(8,128)(2,1)S(1)} %copy-done.37, bf16[256,1536]{1,0:T(8,128)(2,1)S(1)} %copy-done.26), kind=kOutput, calls=%fused_computation.4 | convolution fusion | flops 3638231040 | bytes 9043968 | tf_op jit(solution)/shard_map/dot_general | solution.py:341
  299.1 4.4 fusion.11
  304.6 6.0 %collective-permute-done.47 = bf16[4,192,1152]{2,1,0:T(8,128)(2,1)S(1)} collective-permute-done((bf16[4,192,1152]{2,1,0:T(8,128)(2,1)S(1)}, bf16[4,192,1152]{2,1,0:T(8,128)(2,1)S(1)}, u32[]{:S(2)}, u32[]{:S(2)}) %collective-permute-start.47) | collective-permute-done | bytes 1769504 | tf_op jit(solution)/shard_map/ppermute | solution.py:21
  311.1 3.0 collective-permute-start.52
  318.3 5.4 %collective-permute-done.36 = bf16[256,1536]{1,0:T(8,128)(2,1)S(1)} collective-permute-done((bf16[256,1536]{1,0:T(8,128)(2,1)S(1)}, bf16[256,1536]{1,0:T(8,128)(2,1)S(1)}, u32[]{:S(2)}, u32[]{:S(2)}) %collective-permute-start.36) | collective-permute-done | bytes 786464 | tf_op jit(solution)/shard_map/ppermute | solution.py:21
  328.7 18.3 %collective-permute-done.53 = bf16[192,1152]{1,0:T(8,128)(2,1)S(1)} collective-permute-done((bf16[192,1152]{1,0:T(8,128)(2,1)S(1)}, bf16[192,1152]{1,0:T(8,128)(2,1)S(1)}, u32[]{:S(2)}, u32[]{:S(2)}) %collective-permute-start.53) | collective-permute-done | bytes 442400 | tf_op jit(solution)/shard_map/ppermute | solution.py:21
  350.1 4.1 collective-permute-done.48
  369.3 15.6 %attend_backward.1 = (bf16[1024,384]{1,0:T(8,128)(2,1)S(1)}, bf16[1024,256]{1,0:T(8,128)(2,1)S(1)}, f32[1024,256]{1,0:T(8,128)S(1)}) custom-call(s32[4]{0:T(128)S(1)} %broadcast_xor_fusion.blocks_ref, bf16[1024,384]{1,0:T(8,128)(2,1)S(1)} %copy-done.1, bf16[1024,256]{1,0:T(8,128)(2,1)S(1)} %collective-permute-done.14.prev_ref, ...), custom_call_target="tpu_custom_call" | custom-call | flops 4026531840 | bytes 10485760 | tf_op jit(solution)/shard_map/attend_backward/pallas_call | solution.py:289
  389.2 3.5 convolution_convert_fusion.3
  393.8 18.9 %collective-permute-done.42 = bf16[1024,256]{1,0:T(8,128)(2,1)S(1)} collective-permute-done((bf16[1024,256]{1,0:T(8,128)(2,1)S(1)}, bf16[1024,256]{1,0:T(8,128)(2,1)S(1)}, u32[]{:S(2)}, u32[]{:S(2)}) %collective-permute-start.42) | collective-permute-done | bytes 524320 | tf_op jit(solution)/shard_map/ppermute | solution.py:27
  412.8 2.7 multiply_reduce_fusion.2
  429.7 3.4 collective-permute-done.46
  434.8 3.7 convolution_add_fusion.3
  438.6 10.0 %collective-permute-done.58 = bf16[192,1152]{1,0:T(8,128)(2,1)S(1)} collective-permute-done((bf16[192,1152]{1,0:T(8,128)(2,1)S(1)}, bf16[192,1152]{1,0:T(8,128)(2,1)S(1)}, u32[]{:S(2)}, u32[]{:S(2)}) %collective-permute-start.58) | collective-permute-done | bytes 442400 | tf_op jit(solution)/shard_map/ppermute | solution.py:21
  449.3 12.0 %collective-permute-done.59 = bf16[192,1152]{1,0:T(8,128)(2,1)S(1)} collective-permute-done((bf16[192,1152]{1,0:T(8,128)(2,1)S(1)}, bf16[192,1152]{1,0:T(8,128)(2,1)S(1)}, u32[]{:S(2)}, u32[]{:S(2)}) %collective-permute-start.59) | collective-permute-done | bytes 442400 | tf_op jit(solution)/shard_map/ppermute | solution.py:21
  462.6 9.4 %collective-permute-start.61 = (bf16[192,384]{1,0:T(8,128)(2,1)S(1)}, bf16[192,384]{1,0:T(8,128)(2,1)S(1)}, u32[]{:S(2)}, u32[]{:S(2)}) collective-permute-start(bf16[192,384]{1,0:T(8,128)(2,1)S(1)} %get-tuple-element.67), channel_id=1, source_target_pairs={{0,8},{8,0},{16,24},{24,16},{1,9},{9,1},{17,25},{25,17},{2,10},{10... | collective-permute-start | bytes 442376 | tf_op jit(solution)/shard_map/ppermute | solution.py:21
  472.0 2.4 collective-permute-start.63
  477.3 7.9 %collective-permute-done.62 = bf16[192,384]{1,0:T(8,128)(2,1)S(1)} collective-permute-done((bf16[192,384]{1,0:T(8,128)(2,1)S(1)}, bf16[192,384]{1,0:T(8,128)(2,1)S(1)}, u32[]{:S(2)}, u32[]{:S(2)}) %collective-permute-start.62) | collective-permute-done | bytes 147488 | tf_op jit(solution)/shard_map/ppermute | solution.py:21
  487.3 4.4 collective-permute-done.51
  494.0 2.4 collective-permute-start.66
  500.6 6.7 %collective-permute-done.65 = bf16[240,384]{1,0:T(8,128)(2,1)S(1)} collective-permute-done((bf16[240,384]{1,0:T(8,128)(2,1)S(1)}, bf16[240,384]{1,0:T(8,128)(2,1)S(1)}, u32[]{:S(2)}, u32[]{:S(2)}) %collective-permute-start.65) | collective-permute-done | bytes 184352 | tf_op jit(solution)/shard_map/ppermute | solution.py:21
  (328 shorter events, 121.6 us)
Async XLA Ops:
  5.5 15.7 %collective-permute-start.3 = (bf16[1,48,384]{2,1,0:T(8,128)(2,1)S(1)}, bf16[1,48,384]{2,1,0:T(8,128)(2,1)S(1)}, u32[]{:S(2)}, u32[]{:S(2)}) collective-permute-start(bf16[1,48,384]{2,1,0:T(8,128)(2,1)S(1)} %get-tuple-element.113), channel_id=1, source_target_pairs={{0,2},{1,3},{2,0},{3,1},{4,6},{5,7},{6,4},{7,5},{8,10},{9,11},{10,... | collective-permute-start | bytes 110600 | tf_op jit(solution)/shard_map/ppermute | solution.py:21
  8.5 15.4 %collective-permute-start.6 = (bf16[192,384]{1,0:T(8,128)(2,1)}, bf16[192,384]{1,0:T(8,128)(2,1)S(1)}, u32[]{:S(2)}, u32[]{:S(2)}) collective-permute-start(bf16[192,384]{1,0:T(8,128)(2,1)} %bitcast.300), channel_id=1, source_target_pairs={{0,8},{8,0},{16,24},{24,16},{1,9},{9,1},{17,25},{25,17},{2,10},{10... | collective-permute-start | bytes 442376 | tf_op jit(solution)/shard_map/ppermute | solution.py:21
  21.2 37.9 %collective-permute-start = (bf16[256,1536]{1,0:T(8,128)(2,1)}, bf16[256,1536]{1,0:T(8,128)(2,1)S(1)}, u32[]{:S(2)}, u32[]{:S(2)}) collective-permute-start(bf16[256,1536]{1,0:T(8,128)(2,1)} %bitcast.264), channel_id=1, source_target_pairs={{0,2},{1,3},{2,0},{3,1},{4,6},{5,7},{6,4},{7,5},{8,10},{9,11},{10,... | collective-permute-start | bytes 2359304 | tf_op jit(solution)/shard_map/ppermute | solution.py:21
  22.8 66.3 %collective-permute-start.1 = (bf16[256,1536]{1,0:T(8,128)(2,1)}, bf16[256,1536]{1,0:T(8,128)(2,1)S(1)}, u32[]{:S(2)}, u32[]{:S(2)}) collective-permute-start(bf16[256,1536]{1,0:T(8,128)(2,1)} %bitcast.265), channel_id=1, source_target_pairs={{0,1},{1,0},{2,3},{3,2},{4,5},{5,4},{6,7},{7,6},{8,9},{9,8},{10,11... | collective-permute-start | bytes 2359304 | tf_op jit(solution)/shard_map/ppermute | solution.py:21
  24.3 15.0 %collective-permute-start.9 = (bf16[192,768]{1,0:T(8,128)(2,1)S(1)}, bf16[192,768]{1,0:T(8,128)(2,1)S(1)}, u32[]{:S(2)}, u32[]{:S(2)}) collective-permute-start(bf16[192,768]{1,0:T(8,128)(2,1)S(1)} %pad_maximum_fusion.4), channel_id=1, source_target_pairs={{0,8},{8,0},{16,24},{24,16},{1,9},{9,1},{17,25},{25,17},{2,10},{10... | collective-permute-start | bytes 884744 | tf_op jit(solution)/shard_map/ppermute | solution.py:21
  27.4 23.5 %collective-permute-start.10 = (bf16[192,768]{1,0:T(8,128)(2,1)S(1)}, bf16[192,768]{1,0:T(8,128)(2,1)S(1)}, u32[]{:S(2)}, u32[]{:S(2)}) collective-permute-start(bf16[192,768]{1,0:T(8,128)(2,1)S(1)} %pad_maximum_fusion.4), channel_id=1, source_target_pairs={{0,16},{8,24},{16,0},{24,8},{1,17},{9,25},{17,1},{25,9},{2,18},{10... | collective-permute-start | bytes 884744 | tf_op jit(solution)/shard_map/ppermute | solution.py:21
  28.5 22.4 %collective-permute-start.11 = (bf16[192,768]{1,0:T(8,128)(2,1)S(1)}, bf16[192,768]{1,0:T(8,128)(2,1)S(1)}, u32[]{:S(2)}, u32[]{:S(2)}) collective-permute-start(bf16[192,768]{1,0:T(8,128)(2,1)S(1)} %pad_maximum_fusion.4), channel_id=1, source_target_pairs={{0,24},{8,16},{16,8},{24,0},{1,25},{9,17},{17,9},{25,1},{2,26},{10... | collective-permute-start | bytes 884744 | tf_op jit(solution)/shard_map/ppermute | solution.py:21
  53.3 19.2 %collective-permute-start.20 = (bf16[192,1152]{1,0:T(8,128)(2,1)S(1)}, bf16[192,1152]{1,0:T(8,128)(2,1)S(1)}, u32[]{:S(2)}, u32[]{:S(2)}) collective-permute-start(bf16[192,1152]{1,0:T(8,128)(2,1)S(1)} %copy-done.28), channel_id=1, source_target_pairs={{0,8},{8,0},{16,24},{24,16},{1,9},{9,1},{17,25},{25,17},{2,10},{10... | collective-permute-start | bytes 1327112 | tf_op jit(solution)/shard_map/ppermute | solution.py:21
  56.0 33.0 %collective-permute-start.21 = (bf16[192,1152]{1,0:T(8,128)(2,1)S(1)}, bf16[192,1152]{1,0:T(8,128)(2,1)S(1)}, u32[]{:S(2)}, u32[]{:S(2)}) collective-permute-start(bf16[192,1152]{1,0:T(8,128)(2,1)S(1)} %copy-done.28), channel_id=1, source_target_pairs={{0,16},{8,24},{16,0},{24,8},{1,17},{9,25},{17,1},{25,9},{2,18},{10... | collective-permute-start | bytes 1327112 | tf_op jit(solution)/shard_map/ppermute | solution.py:21
  57.4 31.7 %collective-permute-start.22 = (bf16[192,1152]{1,0:T(8,128)(2,1)S(1)}, bf16[192,1152]{1,0:T(8,128)(2,1)S(1)}, u32[]{:S(2)}, u32[]{:S(2)}) collective-permute-start(bf16[192,1152]{1,0:T(8,128)(2,1)S(1)} %copy-done.28), channel_id=1, source_target_pairs={{0,24},{8,16},{16,8},{24,0},{1,25},{9,17},{17,9},{25,1},{2,26},{10... | collective-permute-start | bytes 1327112 | tf_op jit(solution)/shard_map/ppermute | solution.py:21
  59.1 32.2 %collective-permute-start.13 = (bf16[4,192,768]{2,1,0:T(8,128)(2,1)S(1)}, bf16[4,192,768]{2,1,0:T(8,128)(2,1)S(1)}, u32[]{:S(2)}, u32[]{:S(2)}) collective-permute-start(bf16[4,192,768]{2,1,0:T(8,128)(2,1)S(1)} %bitcast_dynamic-update-slice_fusion.22), channel_id=1, source_target_pairs={{0,4},{4,0},{1,5},{5,1},{2,6},{6,2},{3,7},{7,3},{8,12},{12,8},{9,1... | collective-permute-start | bytes 3538952 | tf_op jit(solution)/shard_map/ppermute | solution.py:21
  72.5 16.6 %collective-permute-start.2 = (bf16[256,1536]{1,0:T(8,128)(2,1)S(1)}, bf16[256,1536]{1,0:T(8,128)(2,1)S(1)}, u32[]{:S(2)}, u32[]{:S(2)}) collective-permute-start(bf16[256,1536]{1,0:T(8,128)(2,1)S(1)} %collective-permute-done), channel_id=1, source_target_pairs={{0,1},{1,0},{2,3},{3,2},{4,5},{5,4},{6,7},{7,6},{8,9},{9,8},{10,11... | collective-permute-start | bytes 2359304 | tf_op jit(solution)/shard_map/ppermute | solution.py:21
  90.2 34.6 %collective-permute-start.28 = (bf16[256,1536]{1,0:T(8,128)(2,1)S(1)}, bf16[256,1536]{1,0:T(8,128)(2,1)S(1)}, u32[]{:S(2)}, u32[]{:S(2)}) collective-permute-start(bf16[256,1536]{1,0:T(8,128)(2,1)S(1)} %bitcast.287), channel_id=1, source_target_pairs={{0,2},{1,3},{2,0},{3,1},{4,6},{5,7},{6,4},{7,5},{8,10},{9,11},{10,... | collective-permute-start | bytes 2359304 | tf_op jit(solution)/shard_map/ppermute | solution.py:21
  91.1 70.4 %collective-permute-start.29 = (bf16[256,1536]{1,0:T(8,128)(2,1)S(1)}, bf16[256,1536]{1,0:T(8,128)(2,1)S(1)}, u32[]{:S(2)}, u32[]{:S(2)}) collective-permute-start(bf16[256,1536]{1,0:T(8,128)(2,1)S(1)} %bitcast.288), channel_id=1, source_target_pairs={{0,1},{1,0},{2,3},{3,2},{4,5},{5,4},{6,7},{7,6},{8,9},{9,8},{10,11... | collective-permute-start | bytes 2359304 | tf_op jit(solution)/shard_map/ppermute | solution.py:21
  91.2 27.6 %collective-permute-start.24 = (bf16[192,1152]{1,0:T(8,128)(2,1)S(1)}, bf16[192,1152]{1,0:T(8,128)(2,1)S(1)}, u32[]{:S(2)}, u32[]{:S(2)}) collective-permute-start(bf16[192,1152]{1,0:T(8,128)(2,1)S(1)} %copy-done.29), channel_id=1, source_target_pairs={{0,8},{8,0},{16,24},{24,16},{1,9},{9,1},{17,25},{25,17},{2,10},{10... | collective-permute-start | bytes 1327112 | tf_op jit(solution)/shard_map/ppermute | solution.py:21
  98.7 22.8 %collective-permute-start.25 = (bf16[192,1152]{1,0:T(8,128)(2,1)S(1)}, bf16[192,1152]{1,0:T(8,128)(2,1)S(1)}, u32[]{:S(2)}, u32[]{:S(2)}) collective-permute-start(bf16[192,1152]{1,0:T(8,128)(2,1)S(1)} %copy-done.29), channel_id=1, source_target_pairs={{0,16},{8,24},{16,0},{24,8},{1,17},{9,25},{17,1},{25,9},{2,18},{10... | collective-permute-start | bytes 1327112 | tf_op jit(solution)/shard_map/ppermute | solution.py:21
  99.7 62.8 %collective-permute-start.23 = (bf16[4,192,1152]{2,1,0:T(8,128)(2,1)S(1)}, bf16[4,192,1152]{2,1,0:T(8,128)(2,1)S(1)}, u32[]{:S(2)}, u32[]{:S(2)}) collective-permute-start(bf16[4,192,1152]{2,1,0:T(8,128)(2,1)S(1)} %bitcast_dynamic-update-slice_fusion.18), channel_id=1, source_target_pairs={{0,4},{4,0},{1,5},{5,1},{2,6},{6,2},{3,7},{7,3},{8,12},{12,8},{9,1... | collective-permute-start | bytes 5308424 | tf_op jit(solution)/shard_map/ppermute | solution.py:21
  121.5 29.1 %collective-permute-start.14 = (bf16[1024,256]{1,0:T(8,128)(2,1)S(1)}, bf16[1024,256]{1,0:T(8,128)(2,1)S(1)}, u32[]{:S(2)}, u32[]{:S(2)}) collective-permute-start(bf16[1024,256]{1,0:T(8,128)(2,1)S(1)} %convolution_convert_fusion.8.own_ref), channel_id=1, source_target_pairs={{0,4},{1,5},{2,6},{3,7},{8,12},{9,13},{10,14},{11,15},{16,20},{17,... | collective-permute-start | bytes 1572872 | tf_op jit(solution)/shard_map/ppermute | solution.py:27
  124.8 37.6 %collective-permute-start.30 = (bf16[256,1536]{1,0:T(8,128)(2,1)S(1)}, bf16[256,1536]{1,0:T(8,128)(2,1)S(1)}, u32[]{:S(2)}, u32[]{:S(2)}) collective-permute-start(bf16[256,1536]{1,0:T(8,128)(2,1)S(1)} %collective-permute-done.28), channel_id=1, source_target_pairs={{0,1},{1,0},{2,3},{3,2},{4,5},{5,4},{6,7},{7,6},{8,9},{9,8},{10,11... | collective-permute-start | bytes 2359304 | tf_op jit(solution)/shard_map/ppermute | solution.py:21
  162.7 19.7 %collective-permute-start.31 = (bf16[192,1152]{1,0:T(8,128)(2,1)S(1)}, bf16[192,1152]{1,0:T(8,128)(2,1)S(1)}, u32[]{:S(2)}, u32[]{:S(2)}) collective-permute-start(bf16[192,1152]{1,0:T(8,128)(2,1)S(1)} %bitcast.296), channel_id=1, source_target_pairs={{0,8},{8,0},{16,24},{24,16},{1,9},{9,1},{17,25},{25,17},{2,10},{10... | collective-permute-start | bytes 1327112 | tf_op jit(solution)/shard_map/ppermute | solution.py:21
  164.4 33.0 %collective-permute-start.32 = (bf16[192,1152]{1,0:T(8,128)(2,1)S(1)}, bf16[192,1152]{1,0:T(8,128)(2,1)S(1)}, u32[]{:S(2)}, u32[]{:S(2)}) collective-permute-start(bf16[192,1152]{1,0:T(8,128)(2,1)S(1)} %bitcast.297), channel_id=1, source_target_pairs={{0,16},{8,24},{16,0},{24,8},{1,17},{9,25},{17,1},{25,9},{2,18},{10... | collective-permute-start | bytes 1327112 | tf_op jit(solution)/shard_map/ppermute | solution.py:21
  164.7 32.7 %collective-permute-start.33 = (bf16[192,1152]{1,0:T(8,128)(2,1)S(1)}, bf16[192,1152]{1,0:T(8,128)(2,1)S(1)}, u32[]{:S(2)}, u32[]{:S(2)}) collective-permute-start(bf16[192,1152]{1,0:T(8,128)(2,1)S(1)} %bitcast.298), channel_id=1, source_target_pairs={{0,24},{8,16},{16,8},{24,0},{1,25},{9,17},{17,9},{25,1},{2,26},{10... | collective-permute-start | bytes 1327112 | tf_op jit(solution)/shard_map/ppermute | solution.py:21
  167.1 40.0 %collective-permute-start.27 = (bf16[4,192,1152]{2,1,0:T(8,128)(2,1)S(1)}, bf16[4,192,1152]{2,1,0:T(8,128)(2,1)S(1)}, u32[]{:S(2)}, u32[]{:S(2)}) collective-permute-start(bf16[4,192,1152]{2,1,0:T(8,128)(2,1)S(1)} %bitcast_dynamic-update-slice_fusion.14), channel_id=1, source_target_pairs={{0,4},{4,0},{1,5},{5,1},{2,6},{6,2},{3,7},{7,3},{8,12},{12,8},{9,1... | collective-permute-start | bytes 5308424 | tf_op jit(solution)/shard_map/ppermute | solution.py:21
  171.7 18.0 %collective-permute-start.16 = (bf16[256,1536]{1,0:T(8,128)(2,1)S(1)}, bf16[256,1536]{1,0:T(8,128)(2,1)S(1)}, u32[]{:S(2)}, u32[]{:S(2)}) collective-permute-start(bf16[256,1536]{1,0:T(8,128)(2,1)S(1)} %slice.263), channel_id=1, source_target_pairs={{0,2},{1,3},{2,0},{3,1},{4,6},{5,7},{6,4},{7,5},{8,10},{9,11},{10,... | collective-permute-start | bytes 2359304 | tf_op jit(solution)/shard_map/ppermute | solution.py:21
  190.4 18.5 %collective-permute-start.17 = (bf16[256,1536]{1,0:T(8,128)(2,1)S(1)}, bf16[256,1536]{1,0:T(8,128)(2,1)S(1)}, u32[]{:S(2)}, u32[]{:S(2)}) collective-permute-start(bf16[256,1536]{1,0:T(8,128)(2,1)S(1)} %multiply_convert_fusion.2), channel_id=1, source_target_pairs={{0,2},{1,3},{2,0},{3,1},{4,6},{5,7},{6,4},{7,5},{8,10},{9,11},{10,... | collective-permute-start | bytes 2359304 | tf_op jit(solution)/shard_map/ppermute | solution.py:21
  207.1 38.6 %collective-permute-start.34 = (bf16[4,192,1152]{2,1,0:T(8,128)(2,1)S(1)}, bf16[4,192,1152]{2,1,0:T(8,128)(2,1)S(1)}, u32[]{:S(2)}, u32[]{:S(2)}) collective-permute-start(bf16[4,192,1152]{2,1,0:T(8,128)(2,1)S(1)} %bitcast_dynamic-update-slice_fusion.10), channel_id=1, source_target_pairs={{0,4},{4,0},{1,5},{5,1},{2,6},{6,2},{3,7},{7,3},{8,12},{12,8},{9,1... | collective-permute-start | bytes 5308424 | tf_op jit(solution)/shard_map/ppermute | solution.py:21
  272.8 37.8 %collective-permute-start.47 = (bf16[4,192,1152]{2,1,0:T(8,128)(2,1)S(1)}, bf16[4,192,1152]{2,1,0:T(8,128)(2,1)S(1)}, u32[]{:S(2)}, u32[]{:S(2)}) collective-permute-start(bf16[4,192,1152]{2,1,0:T(8,128)(2,1)S(1)} %dynamic-slice_bitcast_fusion), channel_id=1, source_target_pairs={{0,4},{4,0},{1,5},{5,1},{2,6},{6,2},{3,7},{7,3},{8,12},{12,8},{9,1... | collective-permute-start | bytes 5308424 | tf_op jit(solution)/shard_map/ppermute | solution.py:21
  278.8 20.3 %collective-permute-start.35 = (bf16[512,1536]{1,0:T(8,128)(2,1)S(1)}, bf16[512,1536]{1,0:T(8,128)(2,1)S(1)}, u32[]{:S(2)}, u32[]{:S(2)}) collective-permute-start(bf16[512,1536]{1,0:T(8,128)(2,1)S(1)} %fusion.12), channel_id=1, source_target_pairs={{0,1},{1,0},{2,3},{3,2},{4,5},{5,4},{6,7},{7,6},{8,9},{9,8},{10,11... | collective-permute-start | bytes 4718600 | tf_op jit(solution)/shard_map/ppermute | solution.py:21
  303.7 20.0 %collective-permute-start.36 = (bf16[256,1536]{1,0:T(8,128)(2,1)S(1)}, bf16[256,1536]{1,0:T(8,128)(2,1)S(1)}, u32[]{:S(2)}, u32[]{:S(2)}) collective-permute-start(bf16[256,1536]{1,0:T(8,128)(2,1)S(1)} %slice.262), channel_id=1, source_target_pairs={{0,2},{1,3},{2,0},{3,1},{4,6},{5,7},{6,4},{7,5},{8,10},{9,11},{10,... | collective-permute-start | bytes 2359304 | tf_op jit(solution)/shard_map/ppermute | solution.py:21
  311.1 17.7 %collective-permute-start.52 = (bf16[192,1152]{1,0:T(8,128)(2,1)S(1)}, bf16[192,1152]{1,0:T(8,128)(2,1)S(1)}, u32[]{:S(2)}, u32[]{:S(2)}) collective-permute-start(bf16[192,1152]{1,0:T(8,128)(2,1)S(1)} %get-tuple-element.119), channel_id=1, source_target_pairs={{0,8},{8,0},{16,24},{24,16},{1,9},{9,1},{17,25},{25,17},{2,10},{10... | collective-permute-start | bytes 1327112 | tf_op jit(solution)/shard_map/ppermute | solution.py:21
  314.1 33.0 %collective-permute-start.53 = (bf16[192,1152]{1,0:T(8,128)(2,1)S(1)}, bf16[192,1152]{1,0:T(8,128)(2,1)S(1)}, u32[]{:S(2)}, u32[]{:S(2)}) collective-permute-start(bf16[192,1152]{1,0:T(8,128)(2,1)S(1)} %get-tuple-element.118), channel_id=1, source_target_pairs={{0,16},{8,24},{16,0},{24,8},{1,17},{9,25},{17,1},{25,9},{2,18},{10... | collective-permute-start | bytes 1327112 | tf_op jit(solution)/shard_map/ppermute | solution.py:21
  314.1 32.9 %collective-permute-start.54 = (bf16[192,1152]{1,0:T(8,128)(2,1)S(1)}, bf16[192,1152]{1,0:T(8,128)(2,1)S(1)}, u32[]{:S(2)}, u32[]{:S(2)}) collective-permute-start(bf16[192,1152]{1,0:T(8,128)(2,1)S(1)} %get-tuple-element.117), channel_id=1, source_target_pairs={{0,24},{8,16},{16,8},{24,0},{1,25},{9,17},{17,9},{25,1},{2,26},{10... | collective-permute-start | bytes 1327112 | tf_op jit(solution)/shard_map/ppermute | solution.py:21
  316.5 37.6 %collective-permute-start.48 = (bf16[4,192,1152]{2,1,0:T(8,128)(2,1)}, bf16[4,192,1152]{2,1,0:T(8,128)(2,1)}, u32[]{:S(2)}, u32[]{:S(2)}) collective-permute-start(bf16[4,192,1152]{2,1,0:T(8,128)(2,1)} %dynamic-slice_bitcast_fusion.1), channel_id=1, source_target_pairs={{0,4},{4,0},{1,5},{5,1},{2,6},{6,2},{3,7},{7,3},{8,12},{12,8},{9,1... | collective-permute-start | bytes 5308424 | tf_op jit(solution)/shard_map/ppermute | solution.py:21
  326.4 23.2 %collective-permute-start.37 = (bf16[256,1536]{1,0:T(8,128)(2,1)}, bf16[256,1536]{1,0:T(8,128)(2,1)}, u32[]{:S(2)}, u32[]{:S(2)}) collective-permute-start(bf16[256,1536]{1,0:T(8,128)(2,1)} %get-tuple-element.106), channel_id=1, source_target_pairs={{0,2},{1,3},{2,0},{3,1},{4,6},{5,7},{6,4},{7,5},{8,10},{9,11},{10,... | collective-permute-start | bytes 2359304 | tf_op jit(solution)/shard_map/ppermute | solution.py:21
  356.7 36.0 %collective-permute-start.55 = (bf16[192,1152]{1,0:T(8,128)(2,1)S(1)}, bf16[192,1152]{1,0:T(8,128)(2,1)S(1)}, u32[]{:S(2)}, u32[]{:S(2)}) collective-permute-start(bf16[192,1152]{1,0:T(8,128)(2,1)S(1)} %get-tuple-element.61), channel_id=1, source_target_pairs={{0,8},{8,0},{16,24},{24,16},{1,9},{9,1},{17,25},{25,17},{2,10},{10... | collective-permute-start | bytes 1327112 | tf_op jit(solution)/shard_map/ppermute | solution.py:21
  358.8 33.9 %collective-permute-start.56 = (bf16[192,1152]{1,0:T(8,128)(2,1)S(1)}, bf16[192,1152]{1,0:T(8,128)(2,1)S(1)}, u32[]{:S(2)}, u32[]{:S(2)}) collective-permute-start(bf16[192,1152]{1,0:T(8,128)(2,1)S(1)} %get-tuple-element.62), channel_id=1, source_target_pairs={{0,16},{8,24},{16,0},{24,8},{1,17},{9,25},{17,1},{25,9},{2,18},{10... | collective-permute-start | bytes 1327112 | tf_op jit(solution)/shard_map/ppermute | solution.py:21
  358.8 33.8 %collective-permute-start.57 = (bf16[192,1152]{1,0:T(8,128)(2,1)S(1)}, bf16[192,1152]{1,0:T(8,128)(2,1)S(1)}, u32[]{:S(2)}, u32[]{:S(2)}) collective-permute-start(bf16[192,1152]{1,0:T(8,128)(2,1)S(1)} %get-tuple-element.63), channel_id=1, source_target_pairs={{0,24},{8,16},{16,8},{24,0},{1,25},{9,17},{17,9},{25,1},{2,26},{10... | collective-permute-start | bytes 1327112 | tf_op jit(solution)/shard_map/ppermute | solution.py:21
  361.2 63.3 %collective-permute-start.49 = (bf16[4,192,1152]{2,1,0:T(8,128)(2,1)}, bf16[4,192,1152]{2,1,0:T(8,128)(2,1)}, u32[]{:S(2)}, u32[]{:S(2)}) collective-permute-start(bf16[4,192,1152]{2,1,0:T(8,128)(2,1)} %dynamic-slice_bitcast_fusion.2), channel_id=1, source_target_pairs={{0,4},{4,0},{1,5},{5,1},{2,6},{6,2},{3,7},{7,3},{8,12},{12,8},{9,1... | collective-permute-start | bytes 5308424 | tf_op jit(solution)/shard_map/ppermute | solution.py:21
  384.9 27.7 %collective-permute-start.42 = (bf16[1024,256]{1,0:T(8,128)(2,1)S(1)}, bf16[1024,256]{1,0:T(8,128)(2,1)S(1)}, u32[]{:S(2)}, u32[]{:S(2)}) collective-permute-start(bf16[1024,256]{1,0:T(8,128)(2,1)S(1)} %get-tuple-element.56), channel_id=1, source_target_pairs={{4,0},{5,1},{6,2},{7,3},{12,8},{13,9},{14,10},{15,11},{20,16},{21,... | collective-permute-start | bytes 1572872 | tf_op jit(solution)/shard_map/ppermute | solution.py:27
  392.7 42.0 %collective-permute-start.40 = (bf16[512,1536]{1,0:T(8,128)(2,1)}, bf16[512,1536]{1,0:T(8,128)(2,1)}, u32[]{:S(2)}, u32[]{:S(2)}) collective-permute-start(bf16[512,1536]{1,0:T(8,128)(2,1)} %convolution_convert_fusion.3), channel_id=1, source_target_pairs={{0,1},{1,0},{2,3},{3,2},{4,5},{5,4},{6,7},{7,6},{8,9},{9,8},{10,11... | collective-permute-start | bytes 4718600 | tf_op jit(solution)/shard_map/ppermute | solution.py:21
  422.7 51.8 %collective-permute-start.43 = (bf16[512,1536]{1,0:T(8,128)(2,1)S(1)}, bf16[512,1536]{1,0:T(8,128)(2,1)S(1)}, u32[]{:S(2)}, u32[]{:S(2)}) collective-permute-start(bf16[512,1536]{1,0:T(8,128)(2,1)S(1)} %fusion.13), channel_id=1, source_target_pairs={{0,1},{1,0},{2,3},{3,2},{4,5},{5,4},{6,7},{7,6},{8,9},{9,8},{10,11... | collective-permute-start | bytes 4718600 | tf_op jit(solution)/shard_map/ppermute | solution.py:21
  427.6 20.9 %collective-permute-start.58 = (bf16[192,1152]{1,0:T(8,128)(2,1)S(1)}, bf16[192,1152]{1,0:T(8,128)(2,1)S(1)}, u32[]{:S(2)}, u32[]{:S(2)}) collective-permute-start(bf16[192,1152]{1,0:T(8,128)(2,1)S(1)} %get-tuple-element.64), channel_id=1, source_target_pairs={{0,8},{8,0},{16,24},{24,16},{1,9},{9,1},{17,25},{25,17},{2,10},{10... | collective-permute-start | bytes 1327112 | tf_op jit(solution)/shard_map/ppermute | solution.py:21
  428.4 32.9 %collective-permute-start.59 = (bf16[192,1152]{1,0:T(8,128)(2,1)S(1)}, bf16[192,1152]{1,0:T(8,128)(2,1)S(1)}, u32[]{:S(2)}, u32[]{:S(2)}) collective-permute-start(bf16[192,1152]{1,0:T(8,128)(2,1)S(1)} %get-tuple-element.65), channel_id=1, source_target_pairs={{0,16},{8,24},{16,0},{24,8},{1,17},{9,25},{17,1},{25,9},{2,18},{10... | collective-permute-start | bytes 1327112 | tf_op jit(solution)/shard_map/ppermute | solution.py:21
  433.1 28.3 %collective-permute-start.60 = (bf16[192,1152]{1,0:T(8,128)(2,1)S(1)}, bf16[192,1152]{1,0:T(8,128)(2,1)S(1)}, u32[]{:S(2)}, u32[]{:S(2)}) collective-permute-start(bf16[192,1152]{1,0:T(8,128)(2,1)S(1)} %get-tuple-element.66), channel_id=1, source_target_pairs={{0,24},{8,16},{16,8},{24,0},{1,25},{9,17},{17,9},{25,1},{2,26},{10... | collective-permute-start | bytes 1327112 | tf_op jit(solution)/shard_map/ppermute | solution.py:21
  434.7 27.7 %collective-permute-start.50 = (bf16[4,192,384]{2,1,0:T(8,128)(2,1)S(1)}, bf16[4,192,384]{2,1,0:T(8,128)(2,1)S(1)}, u32[]{:S(2)}, u32[]{:S(2)}) collective-permute-start(bf16[4,192,384]{2,1,0:T(8,128)(2,1)S(1)} %copy-done.27), channel_id=1, source_target_pairs={{0,4},{4,0},{1,5},{5,1},{2,6},{6,2},{3,7},{7,3},{8,12},{12,8},{9,1... | collective-permute-start | bytes 1769480 | tf_op jit(solution)/shard_map/ppermute | solution.py:21
  448.5 37.5 %collective-permute-start.41 = (bf16[256,1536]{1,0:T(8,128)(2,1)S(1)}, bf16[256,1536]{1,0:T(8,128)(2,1)S(1)}, u32[]{:S(2)}, u32[]{:S(2)}) collective-permute-start(bf16[256,1536]{1,0:T(8,128)(2,1)S(1)} %slice.261), channel_id=1, source_target_pairs={{0,2},{1,3},{2,0},{3,1},{4,6},{5,7},{6,4},{7,5},{8,10},{9,11},{10,... | collective-permute-start | bytes 2359304 | tf_op jit(solution)/shard_map/ppermute | solution.py:21
  474.5 17.2 %collective-permute-start.51 = (bf16[4,240,384]{2,1,0:T(8,128)(2,1)S(1)}, bf16[4,240,384]{2,1,0:T(8,128)(2,1)S(1)}, u32[]{:S(2)}, u32[]{:S(2)}) collective-permute-start(bf16[4,240,384]{2,1,0:T(8,128)(2,1)S(1)} %fusion.44), channel_id=1, source_target_pairs={{0,4},{4,0},{1,5},{5,1},{2,6},{6,2},{3,7},{7,3},{8,12},{12,8},{9,1... | collective-permute-start | bytes 2211848 | tf_op jit(solution)/shard_map/ppermute | solution.py:21
  476.5 19.9 %collective-permute-start.44 = (bf16[256,1536]{1,0:T(8,128)(2,1)S(1)}, bf16[256,1536]{1,0:T(8,128)(2,1)S(1)}, u32[]{:S(2)}, u32[]{:S(2)}) collective-permute-start(bf16[256,1536]{1,0:T(8,128)(2,1)S(1)} %slice.260), channel_id=1, source_target_pairs={{0,2},{1,3},{2,0},{3,1},{4,6},{5,7},{6,4},{7,5},{8,10},{9,11},{10,... | collective-permute-start | bytes 2359304 | tf_op jit(solution)/shard_map/ppermute | solution.py:21
  (68 other events, 947.7 us)
